TPU v7x, 32 devices: a whole 2x2x4 slice. The times are simulated.
32 devices in a mesh: pipe: 4 (over y, x), tensor: 8 (over z, core).
Axes of the slice: x: 2, y: 2, z: 4, core: 2. Of those that a mesh axis runs over, the one named last changes fastest.
Arguments:
- inputs: bfloat16 [8, 128, 8192], P(None, None, 'tensor'), may hold values from -60 to 60
- cotangent: bfloat16 [8, 128, 8192], P(None, None, 'tensor'), may hold values from -13 to 13
- norm_gain: float32 [4, 8192], P('pipe', 'tensor'), may hold values from 0.25 to 1.75
- first_factor: bfloat16 [4, 64, 128, 512], P('pipe', 'tensor'), may hold values from -0.35355339 to 0.35355339
- second_factor: bfloat16 [4, 128, 256, 256], P('pipe', 'tensor'), may hold values from -0.25 to 0.25
- third_factor: bfloat16 [4, 128, 256, 256], P('pipe', 'tensor'), may hold values from -0.3125 to 0.3125
- fourth_factor: bfloat16 [4, 64, 512, 128], P('pipe', 'tensor'), may hold values from -0.22097087 to 0.22097087
Outputs:
- section_out: bfloat16 [4, 8, 128, 8192], P('pipe', None, None, 'tensor')
- section_grad: bfloat16 [4, 8, 128, 8192], P('pipe', None, None, 'tensor')
- gain_grad: float32 [4, 8192], P('pipe', 'tensor')
- first_grad: float32 [4, 64, 128, 512], P('pipe', 'tensor')
- second_grad: float32 [4, 128, 256, 256], P('pipe', 'tensor')
- third_grad: float32 [4, 128, 256, 256], P('pipe', 'tensor')
- fourth_grad: float32 [4, 64, 512, 128], P('pipe', 'tensor')
All inputs are finite; a program needn't handle non-finite values.
Results may differ from a plain program's by a relative error of at most 0.013.
Values may be sent and summed in bfloat16 or wider, within the bound.
A program may use at most 384 MiB of HBM per device.

v0:
```python
import math

import jax
import jax.numpy as jnp
from jax import lax
from jax.sharding import PartitionSpec as P

EPS = 1e-05
TANH_SCALE = math.sqrt(2.0 / math.pi)
CUBIC_COEF = 0.044715


def from_behind(array, axis, by):
    size = lax.axis_size(axis)
    pairs = [(i, i + by) for i in range(size) if 0 <= i + by < size]
    return lax.ppermute(array, axis, pairs)


def gelu_pair(preact):
    tanh_val = jnp.tanh(TANH_SCALE * (preact + CUBIC_COEF * preact * preact * preact))
    gelu_value = 0.5 * preact * (1.0 + tanh_val)
    gelu_slope = 0.5 * (1.0 + tanh_val) + 0.5 * preact * (
        1.0 - tanh_val * tanh_val
    ) * TANH_SCALE * (1.0 + 3.0 * CUBIC_COEF * preact * preact)
    return (gelu_value, gelu_slope)


def row_total(values):
    return lax.psum(values, "tensor")


def to_hidden(values):
    return lax.all_to_all(values, "tensor", split_axis=3, concat_axis=1, tiled=True)


def to_features(values):
    return lax.all_to_all(values, "tensor", split_axis=1, concat_axis=3, tiled=True)


def load_at(stored, micro_slot):
    return lax.dynamic_index_in_dim(stored, micro_slot, 0, keepdims=False)


def store_at(stored, member, micro_slot, is_valid):
    former = lax.dynamic_index_in_dim(stored, micro_slot, 0, keepdims=False)
    return lax.dynamic_update_index_in_dim(
        stored, jnp.where(is_valid, member, former), micro_slot, 0
    )


def body(inputs, cotangent, norm_gain, first_factor, second_factor, third_factor, fourth_factor):
    sections = lax.axis_size("pipe")
    section_id = lax.axis_index("pipe")
    micro_count, tokens, width_dev = inputs.shape
    full_width = width_dev * lax.axis_size("tensor")
    blocks = first_factor.shape[1]
    block_size = first_factor.shape[2]
    expand = first_factor.shape[3] // block_size
    col_blocks = second_factor.shape[1]
    mix_width = second_factor.shape[2]
    all_blocks = mix_width // expand
    gain_row = norm_gain[0]
    factor_one = first_factor[0].reshape(blocks, block_size, expand, block_size)
    factor_two = second_factor[0].reshape(col_blocks, all_blocks, expand, mix_width)
    factor_three = third_factor[0].reshape(col_blocks, mix_width, all_blocks, expand)
    factor_four = fourth_factor[0].reshape(blocks, expand, block_size, block_size)
    ticks = micro_count + sections - 1
    carry = jnp.zeros((tokens, width_dev), jnp.bfloat16)
    out_buffer = jnp.zeros((micro_count, tokens, width_dev), jnp.bfloat16)
    records = None
    for tick_now in range(ticks):
        micro_id = tick_now - section_id
        is_valid = (micro_id >= 0) & (micro_id < micro_count)
        micro_slot = jnp.clip(micro_id, 0, micro_count - 1)
        stream_in = jnp.where(section_id == 0, load_at(inputs, micro_slot), carry)
        forward_stream = stream_in.astype(jnp.float32)
        sum_sq = row_total(jnp.sum(forward_stream * forward_stream, axis=-1))
        forward_inv_rms = lax.rsqrt(sum_sq / full_width + EPS)
        forward_normed = (forward_stream * forward_inv_rms[:, None] * gain_row).astype(jnp.bfloat16)
        spread = jnp.einsum(
            "tij,ijak->tiak",
            forward_normed.reshape(tokens, blocks, block_size),
            factor_one,
            preferred_element_type=jnp.float32,
        ).astype(jnp.bfloat16)
        forward_hidden_in = to_hidden(spread)
        activations_preact = jnp.einsum(
            "tiac,ciae->tce", forward_hidden_in, factor_two, preferred_element_type=jnp.float32
        )
        activations_gelu_value, activations_gelu_slope = gelu_pair(activations_preact)
        middle_activated = activations_gelu_value.astype(jnp.bfloat16)
        mixed_out = jnp.einsum(
            "tce,ceia->tiac", middle_activated, factor_three, preferred_element_type=jnp.float32
        ).astype(jnp.bfloat16)
        forward_feature_in = to_features(mixed_out)
        branch = jnp.einsum(
            "tiak,iakj->tij", forward_feature_in, factor_four, preferred_element_type=jnp.float32
        )
        forward_branch = branch.reshape(forward_feature_in.shape[0], width_dev)
        result = (forward_stream + forward_branch).astype(jnp.bfloat16)
        forward_record = (
            stream_in,
            forward_inv_rms,
            forward_hidden_in,
            forward_feature_in,
            activations_preact,
            middle_activated,
        )
        result, record = (result, forward_record)
        out_buffer = store_at(out_buffer, result, micro_slot, is_valid)
        if records is None:
            records = [jnp.zeros((micro_count,) + member.shape, member.dtype) for member in record]
        records = [
            store_at(stored, member, micro_slot, is_valid)
            for stored, member in zip(records, record)
        ]
        if tick_now + 1 < ticks:
            carry = from_behind(result, "pipe", 1)
    grad_carry = jnp.zeros((tokens, width_dev), jnp.bfloat16)
    grad_buffer = jnp.zeros((micro_count, tokens, width_dev), jnp.bfloat16)
    running = [
        jnp.zeros((width_dev,), jnp.float32),
        jnp.zeros((blocks, block_size, expand, block_size), jnp.float32),
        jnp.zeros((col_blocks, all_blocks, expand, mix_width), jnp.float32),
        jnp.zeros((col_blocks, mix_width, all_blocks, expand), jnp.float32),
        jnp.zeros((blocks, expand, block_size, block_size), jnp.float32),
    ]
    for tick_now in range(ticks):
        micro_id = tick_now - (sections - 1 - section_id)
        is_valid = (micro_id >= 0) & (micro_id < micro_count)
        micro_slot = jnp.clip(micro_id, 0, micro_count - 1)
        grad_out = jnp.where(section_id == sections - 1, load_at(cotangent, micro_slot), grad_carry)
        record = tuple((load_at(stored, micro_slot) for stored in records))
        backward_stream_in, inv_rms, hidden_in, feature_in, preact, activated = record
        stream = backward_stream_in.astype(jnp.float32)
        inv_col = inv_rms[:, None]
        grad_blocks = grad_out.reshape(tokens, blocks, block_size)
        backward_part_four = jnp.einsum(
            "tiak,tij->iakj", feature_in, grad_blocks, preferred_element_type=jnp.float32
        )
        grad_feat = jnp.einsum(
            "tij,iakj->tiak", grad_blocks, factor_four, preferred_element_type=jnp.float32
        ).astype(jnp.bfloat16)
        grad_hidden = to_hidden(grad_feat)
        backward_part_three = jnp.einsum(
            "tce,tiac->ceia", activated, grad_hidden, preferred_element_type=jnp.float32
        )
        grad_act = jnp.einsum(
            "tiac,ceia->tce", grad_hidden, factor_three, preferred_element_type=jnp.float32
        )
        gelu_value, gelu_slope = gelu_pair(preact)
        grad_pre = (grad_act * gelu_slope).astype(jnp.bfloat16)
        backward_part_two = jnp.einsum(
            "tiac,tce->ciae", hidden_in, grad_pre, preferred_element_type=jnp.float32
        )
        grad_mix = jnp.einsum(
            "tce,ciae->tiac", grad_pre, factor_two, preferred_element_type=jnp.float32
        ).astype(jnp.bfloat16)
        grad_spread = to_features(grad_mix)
        normed = (
            (stream * inv_col * gain_row).astype(jnp.bfloat16).reshape(tokens, blocks, block_size)
        )
        backward_part_one = jnp.einsum(
            "tij,tiak->ijak", normed, grad_spread, preferred_element_type=jnp.float32
        )
        grad_norm = jnp.einsum(
            "tiak,ijak->tij", grad_spread, factor_one, preferred_element_type=jnp.float32
        ).reshape(tokens, width_dev)
        backward_part_gain = jnp.sum(grad_norm * stream * inv_col, axis=0)
        scaled_grad = grad_norm * gain_row
        inner_sum = row_total(jnp.sum(scaled_grad * stream, axis=-1))[:, None]
        grad_in = (
            grad_out.astype(jnp.float32)
            + scaled_grad * inv_col
            - stream * inv_col * inv_col * inv_col * inner_sum / full_width
        ).astype(jnp.bfloat16)
        grad_in, parts = (
            grad_in,
            (
                backward_part_gain,
                backward_part_one,
                backward_part_two,
                backward_part_three,
                backward_part_four,
            ),
        )
        running = [
            total + jnp.where(is_valid, member, 0.0) for total, member in zip(running, parts)
        ]
        grad_buffer = store_at(grad_buffer, grad_in, micro_slot, is_valid)
        if tick_now + 1 < ticks:
            grad_carry = from_behind(grad_in, "pipe", -1)
    part_gain, part_one, part_two, part_three, part_four = running
    return (
        out_buffer[None],
        grad_buffer[None],
        part_gain[None],
        part_one.reshape(1, blocks, block_size, expand * block_size),
        part_two.reshape(1, col_blocks, mix_width, mix_width),
        part_three.reshape(1, col_blocks, mix_width, mix_width),
        part_four.reshape(1, blocks, expand * block_size, block_size),
    )


def solution(mesh):
    placed = (
        P(None, None, "tensor"),
        P(None, None, "tensor"),
        P("pipe", "tensor"),
        P("pipe", "tensor", None, None),
        P("pipe", "tensor", None, None),
        P("pipe", "tensor", None, None),
        P("pipe", "tensor", None, None),
    )
    return jax.shard_map(
        body,
        mesh=mesh,
        in_specs=placed,
        out_specs=(
            P("pipe", None, None, "tensor"),
            P("pipe", None, None, "tensor"),
            P("pipe", "tensor"),
            P("pipe", "tensor", None, None),
            P("pipe", "tensor", None, None),
            P("pipe", "tensor", None, None),
            P("pipe", "tensor", None, None),
        ),
        check_vma=False,
    )
```

profile of v0, /device:TPU:0, one launch (start us, length us, event | category | flops | bytes accessed | tf_op | source)
XLA Modules:
  0.0 2329.5 jit_solution(79763381659070703)
XLA Ops:
  6.1 18.1 psum.154
  40.2 19.5 all-to-all-done
  81.1 24.8 %all-to-all-done.1 = bf16[128,64,4,16]{0,2,3,1:T(4,128)(2,1)} async-done(((bf16[128,64,4,16]{0,2,3,1:T(4,128)(2,1)}), bf16[128,64,4,16]{0,2,3,1:T(4,128)(2,1)}, u32[]{:S(2)}, u32[]{:S(2)}) %all-to-all-start.1) | async-done | bytes 1048608 | tf_op jit(solution)/shard_map/all_to_all | solution.py:37
  118.9 14.1 psum.155
  146.1 23.5 %all-to-all-done.2 = bf16[128,8,4,128]{0,2,1,3:T(4,128)(2,1)} async-done(((bf16[128,8,4,128]{0,2,1,3:T(4,128)(2,1)}), bf16[128,8,4,128]{0,2,1,3:T(4,128)(2,1)}, u32[]{:S(2)}, u32[]{:S(2)}) %all-to-all-start.2) | async-done | bytes 1048608 | tf_op jit(solution)/shard_map/all_to_all | solution.py:33
  176.3 29.0 %all_to_all.852 = bf16[128,64,4,16]{0,2,3,1:T(4,128)(2,1)S(1)} all-to-all(bf16[128,64,4,16]{0,2,3,1:T(4,128)(2,1)S(1)} %copy.791), channel_id=1, replica_groups=mesh['pipe'=4,'tensor'=8] {'tensor'}, dimensions={1} | all-to-all | bytes 2097152 | tf_op jit(solution)/shard_map/all_to_all | solution.py:37
  219.2 14.3 psum.156
  246.4 23.5 %all-to-all-done.4 = bf16[128,8,4,128]{0,2,1,3:T(4,128)(2,1)} async-done(((bf16[128,8,4,128]{0,2,1,3:T(4,128)(2,1)}), bf16[128,8,4,128]{0,2,1,3:T(4,128)(2,1)}, u32[]{:S(2)}, u32[]{:S(2)}) %all-to-all-start.4) | async-done | bytes 1048608 | tf_op jit(solution)/shard_map/all_to_all | solution.py:33
  284.0 24.9 %all-to-all-done.5 = bf16[128,64,4,16]{0,2,3,1:T(4,128)(2,1)} async-done(((bf16[128,64,4,16]{0,2,3,1:T(4,128)(2,1)}), bf16[128,64,4,16]{0,2,3,1:T(4,128)(2,1)}, u32[]{:S(2)}, u32[]{:S(2)}) %all-to-all-start.5) | async-done | bytes 1048608 | tf_op jit(solution)/shard_map/all_to_all | solution.py:37
  351.3 23.5 %all-to-all-done.6 = bf16[128,8,4,128]{0,2,1,3:T(4,128)(2,1)} async-done(((bf16[128,8,4,128]{0,2,1,3:T(4,128)(2,1)}), bf16[128,8,4,128]{0,2,1,3:T(4,128)(2,1)}, u32[]{:S(2)}, u32[]{:S(2)}) %all-to-all-start.6) | async-done | bytes 1048608 | tf_op jit(solution)/shard_map/all_to_all | solution.py:33
  388.4 24.9 %all-to-all-done.7 = bf16[128,64,4,16]{0,2,3,1:T(4,128)(2,1)} async-done(((bf16[128,64,4,16]{0,2,3,1:T(4,128)(2,1)}), bf16[128,64,4,16]{0,2,3,1:T(4,128)(2,1)}, u32[]{:S(2)}, u32[]{:S(2)}) %all-to-all-start.7) | async-done | bytes 1048608 | tf_op jit(solution)/shard_map/all_to_all | solution.py:37
  429.6 14.1 psum.158
  456.7 23.5 %all-to-all-done.8 = bf16[128,8,4,128]{0,2,1,3:T(4,128)(2,1)} async-done(((bf16[128,8,4,128]{0,2,1,3:T(4,128)(2,1)}), bf16[128,8,4,128]{0,2,1,3:T(4,128)(2,1)}, u32[]{:S(2)}, u32[]{:S(2)}) %all-to-all-start.8) | async-done | bytes 1048608 | tf_op jit(solution)/shard_map/all_to_all | solution.py:33
  493.9 24.9 %all-to-all-done.9 = bf16[128,64,4,16]{0,2,3,1:T(4,128)(2,1)} async-done(((bf16[128,64,4,16]{0,2,3,1:T(4,128)(2,1)}), bf16[128,64,4,16]{0,2,3,1:T(4,128)(2,1)}, u32[]{:S(2)}, u32[]{:S(2)}) %all-to-all-start.9) | async-done | bytes 1048608 | tf_op jit(solution)/shard_map/all_to_all | solution.py:37
  535.1 14.1 psum.159
  562.2 23.5 %all-to-all-done.10 = bf16[128,8,4,128]{0,2,1,3:T(4,128)(2,1)} async-done(((bf16[128,8,4,128]{0,2,1,3:T(4,128)(2,1)}), bf16[128,8,4,128]{0,2,1,3:T(4,128)(2,1)}, u32[]{:S(2)}, u32[]{:S(2)}) %all-to-all-start.10) | async-done | bytes 1048608 | tf_op jit(solution)/shard_map/all_to_all | solution.py:33
  599.5 24.9 %all-to-all-done.11 = bf16[128,64,4,16]{0,2,3,1:T(4,128)(2,1)} async-done(((bf16[128,64,4,16]{0,2,3,1:T(4,128)(2,1)}), bf16[128,64,4,16]{0,2,3,1:T(4,128)(2,1)}, u32[]{:S(2)}, u32[]{:S(2)}) %all-to-all-start.11) | async-done | bytes 1048608 | tf_op jit(solution)/shard_map/all_to_all | solution.py:37
  640.8 14.1 psum.160
  667.8 23.5 %all-to-all-done.12 = bf16[128,8,4,128]{0,2,1,3:T(4,128)(2,1)} async-done(((bf16[128,8,4,128]{0,2,1,3:T(4,128)(2,1)}), bf16[128,8,4,128]{0,2,1,3:T(4,128)(2,1)}, u32[]{:S(2)}, u32[]{:S(2)}) %all-to-all-start.12) | async-done | bytes 1048608 | tf_op jit(solution)/shard_map/all_to_all | solution.py:33
  704.9 24.9 %all-to-all-done.13 = bf16[128,64,4,16]{0,2,3,1:T(4,128)(2,1)} async-done(((bf16[128,64,4,16]{0,2,3,1:T(4,128)(2,1)}), bf16[128,64,4,16]{0,2,3,1:T(4,128)(2,1)}, u32[]{:S(2)}, u32[]{:S(2)}) %all-to-all-start.13) | async-done | bytes 1048608 | tf_op jit(solution)/shard_map/all_to_all | solution.py:37
  746.2 14.1 psum.161
  773.6 23.5 %all-to-all-done.14 = bf16[128,8,4,128]{0,2,1,3:T(4,128)(2,1)} async-done(((bf16[128,8,4,128]{0,2,1,3:T(4,128)(2,1)}), bf16[128,8,4,128]{0,2,1,3:T(4,128)(2,1)}, u32[]{:S(2)}, u32[]{:S(2)}) %all-to-all-start.14) | async-done | bytes 1048608 | tf_op jit(solution)/shard_map/all_to_all | solution.py:33
  810.7 24.9 %all-to-all-done.15 = bf16[128,64,4,16]{0,2,3,1:T(4,128)(2,1)} async-done(((bf16[128,64,4,16]{0,2,3,1:T(4,128)(2,1)}), bf16[128,64,4,16]{0,2,3,1:T(4,128)(2,1)}, u32[]{:S(2)}, u32[]{:S(2)}) %all-to-all-start.15) | async-done | bytes 1048608 | tf_op jit(solution)/shard_map/all_to_all | solution.py:37
  852.0 14.1 psum.162
  879.0 23.5 %all-to-all-done.16 = bf16[128,8,4,128]{0,2,1,3:T(4,128)(2,1)} async-done(((bf16[128,8,4,128]{0,2,1,3:T(4,128)(2,1)}), bf16[128,8,4,128]{0,2,1,3:T(4,128)(2,1)}, u32[]{:S(2)}, u32[]{:S(2)}) %all-to-all-start.16) | async-done | bytes 1048608 | tf_op jit(solution)/shard_map/all_to_all | solution.py:33
  916.3 24.9 %all-to-all-done.17 = bf16[128,64,4,16]{0,2,3,1:T(4,128)(2,1)} async-done(((bf16[128,64,4,16]{0,2,3,1:T(4,128)(2,1)}), bf16[128,64,4,16]{0,2,3,1:T(4,128)(2,1)}, u32[]{:S(2)}, u32[]{:S(2)}) %all-to-all-start.17) | async-done | bytes 1048608 | tf_op jit(solution)/shard_map/all_to_all | solution.py:37
  984.5 23.5 %all-to-all-done.18 = bf16[128,8,4,128]{0,2,1,3:T(4,128)(2,1)} async-done(((bf16[128,8,4,128]{0,2,1,3:T(4,128)(2,1)}), bf16[128,8,4,128]{0,2,1,3:T(4,128)(2,1)}, u32[]{:S(2)}, u32[]{:S(2)}) %all-to-all-start.18) | async-done | bytes 1048608 | tf_op jit(solution)/shard_map/all_to_all | solution.py:33
  1031.0 15.5 all-to-all-done.19
  1068.7 16.2 psum.164
  1101.6 20.8 all-to-all-done.20
  1141.3 24.1 %all-to-all-done.23 = bf16[128,64,4,16]{0,2,3,1:T(4,128)(2,1)} async-done(((bf16[128,64,4,16]{0,2,3,1:T(4,128)(2,1)}), bf16[128,64,4,16]{0,2,3,1:T(4,128)(2,1)}, u32[]{:S(2)}, u32[]{:S(2)}) %all-to-all-start.23) | async-done | bytes 1048608 | tf_op jit(solution)/shard_map/all_to_all | solution.py:37
  1169.2 14.5 psum.165
  1202.7 30.6 %all_to_all.853 = bf16[128,8,4,128]{0,2,1,3:T(4,128)(2,1)S(1)} all-to-all(bf16[128,8,4,128]{0,2,1,3:T(4,128)(2,1)} %copy.927), channel_id=1, replica_groups=mesh['pipe'=4,'tensor'=8] {'tensor'}, dimensions={3} | all-to-all | bytes 2097152 | tf_op jit(solution)/shard_map/all_to_all | solution.py:33
  1253.4 18.9 all-to-all-done.25
  1276.0 14.5 psum.166
  1309.7 30.4 %all_to_all.854 = bf16[128,8,4,128]{0,2,1,3:T(4,128)(2,1)S(1)} all-to-all(bf16[128,8,4,128]{0,2,1,3:T(4,128)(2,1)} %copy.939), channel_id=1, replica_groups=mesh['pipe'=4,'tensor'=8] {'tensor'}, dimensions={3} | all-to-all | bytes 2097152 | tf_op jit(solution)/shard_map/all_to_all | solution.py:33
  1354.1 24.9 %all-to-all-done.27 = bf16[128,64,4,16]{0,2,3,1:T(4,128)(2,1)} async-done(((bf16[128,64,4,16]{0,2,3,1:T(4,128)(2,1)}), bf16[128,64,4,16]{0,2,3,1:T(4,128)(2,1)}, u32[]{:S(2)}, u32[]{:S(2)}) %all-to-all-start.27) | async-done | bytes 1048608 | tf_op jit(solution)/shard_map/all_to_all | solution.py:37
  1382.8 14.5 psum.167
  1415.8 30.4 %all_to_all.855 = bf16[128,8,4,128]{0,2,1,3:T(4,128)(2,1)S(1)} all-to-all(bf16[128,8,4,128]{0,2,1,3:T(4,128)(2,1)} %copy.951), channel_id=1, replica_groups=mesh['pipe'=4,'tensor'=8] {'tensor'}, dimensions={3} | all-to-all | bytes 2097152 | tf_op jit(solution)/shard_map/all_to_all | solution.py:33
  1460.3 24.9 %all-to-all-done.29 = bf16[128,64,4,16]{0,2,3,1:T(4,128)(2,1)} async-done(((bf16[128,64,4,16]{0,2,3,1:T(4,128)(2,1)}), bf16[128,64,4,16]{0,2,3,1:T(4,128)(2,1)}, u32[]{:S(2)}, u32[]{:S(2)}) %all-to-all-start.29) | async-done | bytes 1048608 | tf_op jit(solution)/shard_map/all_to_all | solution.py:37
  1488.9 14.5 psum.168
  1608.2 14.5 psum.169
  1714.2 14.5 psum.170
  1843.6 17.0 psum.171
  1952.6 14.5 psum.172
  2059.4 14.5 psum.173
  2166.1 14.5 psum.174
  2292.6 17.2 psum.175
  (1090 shorter events, 1348.2 us)
Async XLA Ops:
  28.9 30.8 %all-to-all-start = ((bf16[128,8,4,128]{0,2,1,3:T(4,128)(2,1)}), bf16[128,8,4,128]{0,2,1,3:T(4,128)(2,1)}, u32[]{:S(2)}, u32[]{:S(2)}) async-start(bf16[128,8,4,128]{0,2,1,3:T(4,128)(2,1)} %copy.772), calls=%async_computation | async-start | bytes 2097152 | tf_op jit(solution)/shard_map/all_to_all | solution.py:33
  75.0 30.8 %all-to-all-start.1 = ((bf16[128,64,4,16]{0,2,3,1:T(4,128)(2,1)}), bf16[128,64,4,16]{0,2,3,1:T(4,128)(2,1)}, u32[]{:S(2)}, u32[]{:S(2)}) async-start(bf16[128,64,4,16]{0,2,3,1:T(4,128)(2,1)} %copy.778), calls=%async_computation.1 | async-start | bytes 2097152 | tf_op jit(solution)/shard_map/all_to_all | solution.py:37
  138.5 31.0 %all-to-all-start.2 = ((bf16[128,8,4,128]{0,2,1,3:T(4,128)(2,1)}), bf16[128,8,4,128]{0,2,1,3:T(4,128)(2,1)}, u32[]{:S(2)}, u32[]{:S(2)}) async-start(bf16[128,8,4,128]{0,2,1,3:T(4,128)(2,1)} %copy.786), calls=%async_computation.2 | async-start | bytes 2097152 | tf_op jit(solution)/shard_map/all_to_all | solution.py:33
  239.1 30.8 %all-to-all-start.4 = ((bf16[128,8,4,128]{0,2,1,3:T(4,128)(2,1)}), bf16[128,8,4,128]{0,2,1,3:T(4,128)(2,1)}, u32[]{:S(2)}, u32[]{:S(2)}) async-start(bf16[128,8,4,128]{0,2,1,3:T(4,128)(2,1)} %copy.799), calls=%async_computation.4 | async-start | bytes 2097152 | tf_op jit(solution)/shard_map/all_to_all | solution.py:33
  277.7 31.2 %all-to-all-start.5 = ((bf16[128,64,4,16]{0,2,3,1:T(4,128)(2,1)}), bf16[128,64,4,16]{0,2,3,1:T(4,128)(2,1)}, u32[]{:S(2)}, u32[]{:S(2)}) async-start(bf16[128,64,4,16]{0,2,3,1:T(4,128)(2,1)} %copy.804), calls=%async_computation.5 | async-start | bytes 2097152 | tf_op jit(solution)/shard_map/all_to_all | solution.py:37
  343.9 30.8 %all-to-all-start.6 = ((bf16[128,8,4,128]{0,2,1,3:T(4,128)(2,1)}), bf16[128,8,4,128]{0,2,1,3:T(4,128)(2,1)}, u32[]{:S(2)}, u32[]{:S(2)}) async-start(bf16[128,8,4,128]{0,2,1,3:T(4,128)(2,1)} %copy.812), calls=%async_computation.6 | async-start | bytes 2097152 | tf_op jit(solution)/shard_map/all_to_all | solution.py:33
  382.5 30.8 %all-to-all-start.7 = ((bf16[128,64,4,16]{0,2,3,1:T(4,128)(2,1)}), bf16[128,64,4,16]{0,2,3,1:T(4,128)(2,1)}, u32[]{:S(2)}, u32[]{:S(2)}) async-start(bf16[128,64,4,16]{0,2,3,1:T(4,128)(2,1)} %copy.817), calls=%async_computation.7 | async-start | bytes 2097152 | tf_op jit(solution)/shard_map/all_to_all | solution.py:37
  449.2 31.0 %all-to-all-start.8 = ((bf16[128,8,4,128]{0,2,1,3:T(4,128)(2,1)}), bf16[128,8,4,128]{0,2,1,3:T(4,128)(2,1)}, u32[]{:S(2)}, u32[]{:S(2)}) async-start(bf16[128,8,4,128]{0,2,1,3:T(4,128)(2,1)} %copy.825), calls=%async_computation.8 | async-start | bytes 2097152 | tf_op jit(solution)/shard_map/all_to_all | solution.py:33
  487.9 30.8 %all-to-all-start.9 = ((bf16[128,64,4,16]{0,2,3,1:T(4,128)(2,1)}), bf16[128,64,4,16]{0,2,3,1:T(4,128)(2,1)}, u32[]{:S(2)}, u32[]{:S(2)}) async-start(bf16[128,64,4,16]{0,2,3,1:T(4,128)(2,1)} %copy.830), calls=%async_computation.9 | async-start | bytes 2097152 | tf_op jit(solution)/shard_map/all_to_all | solution.py:37
  522.2 11.0 collective-permute-start.4
  554.8 30.8 %all-to-all-start.10 = ((bf16[128,8,4,128]{0,2,1,3:T(4,128)(2,1)}), bf16[128,8,4,128]{0,2,1,3:T(4,128)(2,1)}, u32[]{:S(2)}, u32[]{:S(2)}) async-start(bf16[128,8,4,128]{0,2,1,3:T(4,128)(2,1)} %copy.838), calls=%async_computation.10 | async-start | bytes 2097152 | tf_op jit(solution)/shard_map/all_to_all | solution.py:33
  593.3 31.1 %all-to-all-start.11 = ((bf16[128,64,4,16]{0,2,3,1:T(4,128)(2,1)}), bf16[128,64,4,16]{0,2,3,1:T(4,128)(2,1)}, u32[]{:S(2)}, u32[]{:S(2)}) async-start(bf16[128,64,4,16]{0,2,3,1:T(4,128)(2,1)} %copy.843), calls=%async_computation.11 | async-start | bytes 2097152 | tf_op jit(solution)/shard_map/all_to_all | solution.py:37
  627.8 11.0 collective-permute-start.5
  660.4 30.8 %all-to-all-start.12 = ((bf16[128,8,4,128]{0,2,1,3:T(4,128)(2,1)}), bf16[128,8,4,128]{0,2,1,3:T(4,128)(2,1)}, u32[]{:S(2)}, u32[]{:S(2)}) async-start(bf16[128,8,4,128]{0,2,1,3:T(4,128)(2,1)} %copy.851), calls=%async_computation.12 | async-start | bytes 2097152 | tf_op jit(solution)/shard_map/all_to_all | solution.py:33
  699.0 30.8 %all-to-all-start.13 = ((bf16[128,64,4,16]{0,2,3,1:T(4,128)(2,1)}), bf16[128,64,4,16]{0,2,3,1:T(4,128)(2,1)}, u32[]{:S(2)}, u32[]{:S(2)}) async-start(bf16[128,64,4,16]{0,2,3,1:T(4,128)(2,1)} %copy.856), calls=%async_computation.13 | async-start | bytes 2097152 | tf_op jit(solution)/shard_map/all_to_all | solution.py:37
  733.2 11.0 collective-permute-start.6
  765.8 31.2 %all-to-all-start.14 = ((bf16[128,8,4,128]{0,2,1,3:T(4,128)(2,1)}), bf16[128,8,4,128]{0,2,1,3:T(4,128)(2,1)}, u32[]{:S(2)}, u32[]{:S(2)}) async-start(bf16[128,8,4,128]{0,2,1,3:T(4,128)(2,1)} %copy.864), calls=%async_computation.14 | async-start | bytes 2097152 | tf_op jit(solution)/shard_map/all_to_all | solution.py:33
  804.7 30.9 %all-to-all-start.15 = ((bf16[128,64,4,16]{0,2,3,1:T(4,128)(2,1)}), bf16[128,64,4,16]{0,2,3,1:T(4,128)(2,1)}, u32[]{:S(2)}, u32[]{:S(2)}) async-start(bf16[128,64,4,16]{0,2,3,1:T(4,128)(2,1)} %copy.869), calls=%async_computation.15 | async-start | bytes 2097152 | tf_op jit(solution)/shard_map/all_to_all | solution.py:37
  839.0 11.1 collective-permute-start.7
  871.6 30.9 %all-to-all-start.16 = ((bf16[128,8,4,128]{0,2,1,3:T(4,128)(2,1)}), bf16[128,8,4,128]{0,2,1,3:T(4,128)(2,1)}, u32[]{:S(2)}, u32[]{:S(2)}) async-start(bf16[128,8,4,128]{0,2,1,3:T(4,128)(2,1)} %copy.877), calls=%async_computation.16 | async-start | bytes 2097152 | tf_op jit(solution)/shard_map/all_to_all | solution.py:33
  910.2 31.0 %all-to-all-start.17 = ((bf16[128,64,4,16]{0,2,3,1:T(4,128)(2,1)}), bf16[128,64,4,16]{0,2,3,1:T(4,128)(2,1)}, u32[]{:S(2)}, u32[]{:S(2)}) async-start(bf16[128,64,4,16]{0,2,3,1:T(4,128)(2,1)} %copy.882), calls=%async_computation.17 | async-start | bytes 2097152 | tf_op jit(solution)/shard_map/all_to_all | solution.py:37
  944.5 11.0 collective-permute-start.8
  977.2 30.8 %all-to-all-start.18 = ((bf16[128,8,4,128]{0,2,1,3:T(4,128)(2,1)}), bf16[128,8,4,128]{0,2,1,3:T(4,128)(2,1)}, u32[]{:S(2)}, u32[]{:S(2)}) async-start(bf16[128,8,4,128]{0,2,1,3:T(4,128)(2,1)} %copy.890), calls=%async_computation.18 | async-start | bytes 2097152 | tf_op jit(solution)/shard_map/all_to_all | solution.py:33
  1015.7 30.8 %all-to-all-start.19 = ((bf16[128,64,4,16]{0,2,3,1:T(4,128)(2,1)}), bf16[128,64,4,16]{0,2,3,1:T(4,128)(2,1)}, u32[]{:S(2)}, u32[]{:S(2)}) async-start(bf16[128,64,4,16]{0,2,3,1:T(4,128)(2,1)} %copy.895), calls=%async_computation.19 | async-start | bytes 2097152 | tf_op jit(solution)/shard_map/all_to_all | solution.py:37
  1046.5 44.8 %all-to-all-start.22 = ((bf16[128,8,4,128]{0,2,1,3:T(4,128)(2,1)}), bf16[128,8,4,128]{0,2,1,3:T(4,128)(2,1)}, u32[]{:S(2)}, u32[]{:S(2)}) async-start(bf16[128,8,4,128]{0,2,1,3:T(4,128)(2,1)} %copy.915), calls=%async_computation.22 | async-start | bytes 2097152 | tf_op jit(solution)/shard_map/all_to_all | solution.py:33
  1054.2 11.8 collective-permute-start.9
  1091.4 31.0 %all-to-all-start.20 = ((bf16[128,8,4,128]{0,2,1,3:T(4,128)(2,1)}), bf16[128,8,4,128]{0,2,1,3:T(4,128)(2,1)}, u32[]{:S(2)}, u32[]{:S(2)}) async-start(bf16[128,8,4,128]{0,2,1,3:T(4,128)(2,1)} %copy.903), calls=%async_computation.20 | async-start | bytes 2097152 | tf_op jit(solution)/shard_map/all_to_all | solution.py:33
  1134.6 30.9 %all-to-all-start.23 = ((bf16[128,64,4,16]{0,2,3,1:T(4,128)(2,1)}), bf16[128,64,4,16]{0,2,3,1:T(4,128)(2,1)}, u32[]{:S(2)}, u32[]{:S(2)}) async-start(bf16[128,64,4,16]{0,2,3,1:T(4,128)(2,1)} %copy.920), calls=%async_computation.23 | async-start | bytes 2097152 | tf_op jit(solution)/shard_map/all_to_all | solution.py:37
  1185.7 11.1 collective-permute-start.10
  1241.4 30.9 %all-to-all-start.25 = ((bf16[128,64,4,16]{0,2,3,1:T(4,128)(2,1)}), bf16[128,64,4,16]{0,2,3,1:T(4,128)(2,1)}, u32[]{:S(2)}, u32[]{:S(2)}) async-start(bf16[128,64,4,16]{0,2,3,1:T(4,128)(2,1)} %copy.932), calls=%async_computation.25 | async-start | bytes 2097152 | tf_op jit(solution)/shard_map/all_to_all | solution.py:37
  1292.8 11.0 collective-permute-start.11
  1348.2 30.9 %all-to-all-start.27 = ((bf16[128,64,4,16]{0,2,3,1:T(4,128)(2,1)}), bf16[128,64,4,16]{0,2,3,1:T(4,128)(2,1)}, u32[]{:S(2)}, u32[]{:S(2)}) async-start(bf16[128,64,4,16]{0,2,3,1:T(4,128)(2,1)} %copy.944), calls=%async_computation.27 | async-start | bytes 2097152 | tf_op jit(solution)/shard_map/all_to_all | solution.py:37
  1454.3 30.9 %all-to-all-start.29 = ((bf16[128,64,4,16]{0,2,3,1:T(4,128)(2,1)}), bf16[128,64,4,16]{0,2,3,1:T(4,128)(2,1)}, u32[]{:S(2)}, u32[]{:S(2)}) async-start(bf16[128,64,4,16]{0,2,3,1:T(4,128)(2,1)} %copy.956), calls=%async_computation.29 | async-start | bytes 2097152 | tf_op jit(solution)/shard_map/all_to_all | solution.py:37
  1522.0 40.9 %all-to-all-start.30 = ((bf16[128,8,4,128]{0,2,1,3:T(4,128)(2,1)}), bf16[128,8,4,128]{0,2,1,3:T(4,128)(2,1)}, u32[]{:S(2)}, u32[]{:S(2)}) async-start(bf16[128,8,4,128]{0,2,1,3:T(4,128)(2,1)} %copy.963), calls=%async_computation.30 | async-start | bytes 2097152 | tf_op jit(solution)/shard_map/all_to_all | solution.py:33
  1572.2 32.2 %all-to-all-start.31 = ((bf16[128,64,4,16]{0,2,3,1:T(4,128)(2,1)}), bf16[128,64,4,16]{0,2,3,1:T(4,128)(2,1)}, u32[]{:S(2)}, u32[]{:S(2)}) async-start(bf16[128,64,4,16]{0,2,3,1:T(4,128)(2,1)} %copy.968), calls=%async_computation.31 | async-start | bytes 2097152 | tf_op jit(solution)/shard_map/all_to_all | solution.py:37
  1639.0 31.0 %all-to-all-start.32 = ((bf16[128,8,4,128]{0,2,1,3:T(4,128)(2,1)}), bf16[128,8,4,128]{0,2,1,3:T(4,128)(2,1)}, u32[]{:S(2)}, u32[]{:S(2)}) async-start(bf16[128,8,4,128]{0,2,1,3:T(4,128)(2,1)} %copy.975), calls=%async_computation.32 | async-start | bytes 2097152 | tf_op jit(solution)/shard_map/all_to_all | solution.py:33
  1679.4 31.0 %all-to-all-start.33 = ((bf16[128,64,4,16]{0,2,3,1:T(4,128)(2,1)}), bf16[128,64,4,16]{0,2,3,1:T(4,128)(2,1)}, u32[]{:S(2)}, u32[]{:S(2)}) async-start(bf16[128,64,4,16]{0,2,3,1:T(4,128)(2,1)} %copy.980), calls=%async_computation.33 | async-start | bytes 2097152 | tf_op jit(solution)/shard_map/all_to_all | solution.py:37
  1745.5 31.3 %all-to-all-start.34 = ((bf16[128,8,4,128]{0,2,1,3:T(4,128)(2,1)}), bf16[128,8,4,128]{0,2,1,3:T(4,128)(2,1)}, u32[]{:S(2)}, u32[]{:S(2)}) async-start(bf16[128,8,4,128]{0,2,1,3:T(4,128)(2,1)} %copy.987), calls=%async_computation.34 | async-start | bytes 2097152 | tf_op jit(solution)/shard_map/all_to_all | solution.py:33
  1786.2 31.0 %all-to-all-start.35 = ((bf16[128,64,4,16]{0,2,3,1:T(4,128)(2,1)}), bf16[128,64,4,16]{0,2,3,1:T(4,128)(2,1)}, u32[]{:S(2)}, u32[]{:S(2)}) async-start(bf16[128,64,4,16]{0,2,3,1:T(4,128)(2,1)} %copy.992), calls=%async_computation.35 | async-start | bytes 2097152 | tf_op jit(solution)/shard_map/all_to_all | solution.py:37
  1817.2 51.4 %all-to-all-start.21 = ((bf16[128,64,4,16]{0,2,3,1:T(4,128)(2,1)}), bf16[128,64,4,16]{0,2,3,1:T(4,128)(2,1)}, u32[]{:S(2)}, u32[]{:S(2)}) async-start(bf16[128,64,4,16]{0,2,3,1:T(4,128)(2,1)} %copy.908), calls=%async_computation.21 | async-start | bytes 2097152 | tf_op jit(solution)/shard_map/all_to_all | solution.py:37
  1877.9 30.8 %all-to-all-start.36 = ((bf16[128,8,4,128]{0,2,1,3:T(4,128)(2,1)}), bf16[128,8,4,128]{0,2,1,3:T(4,128)(2,1)}, u32[]{:S(2)}, u32[]{:S(2)}) async-start(bf16[128,8,4,128]{0,2,1,3:T(4,128)(2,1)} %copy.999), calls=%async_computation.36 | async-start | bytes 2097152 | tf_op jit(solution)/shard_map/all_to_all | solution.py:33
  1918.2 31.2 %all-to-all-start.37 = ((bf16[128,64,4,16]{0,2,3,1:T(4,128)(2,1)}), bf16[128,64,4,16]{0,2,3,1:T(4,128)(2,1)}, u32[]{:S(2)}, u32[]{:S(2)}) async-start(bf16[128,64,4,16]{0,2,3,1:T(4,128)(2,1)} %copy.1004), calls=%async_computation.37 | async-start | bytes 2097152 | tf_op jit(solution)/shard_map/all_to_all | solution.py:37
  1984.6 31.0 %all-to-all-start.38 = ((bf16[128,8,4,128]{0,2,1,3:T(4,128)(2,1)}), bf16[128,8,4,128]{0,2,1,3:T(4,128)(2,1)}, u32[]{:S(2)}, u32[]{:S(2)}) async-start(bf16[128,8,4,128]{0,2,1,3:T(4,128)(2,1)} %copy.1011), calls=%async_computation.38 | async-start | bytes 2097152 | tf_op jit(solution)/shard_map/all_to_all | solution.py:33
  2025.1 31.1 %all-to-all-start.39 = ((bf16[128,64,4,16]{0,2,3,1:T(4,128)(2,1)}), bf16[128,64,4,16]{0,2,3,1:T(4,128)(2,1)}, u32[]{:S(2)}, u32[]{:S(2)}) async-start(bf16[128,64,4,16]{0,2,3,1:T(4,128)(2,1)} %copy.1016), calls=%async_computation.39 | async-start | bytes 2097152 | tf_op jit(solution)/shard_map/all_to_all | solution.py:37
  2091.1 31.1 %all-to-all-start.40 = ((bf16[128,8,4,128]{0,2,1,3:T(4,128)(2,1)}), bf16[128,8,4,128]{0,2,1,3:T(4,128)(2,1)}, u32[]{:S(2)}, u32[]{:S(2)}) async-start(bf16[128,8,4,128]{0,2,1,3:T(4,128)(2,1)} %copy.1023), calls=%async_computation.40 | async-start | bytes 2097152 | tf_op jit(solution)/shard_map/all_to_all | solution.py:33
  2131.6 31.3 %all-to-all-start.41 = ((bf16[128,64,4,16]{0,2,3,1:T(4,128)(2,1)}), bf16[128,64,4,16]{0,2,3,1:T(4,128)(2,1)}, u32[]{:S(2)}, u32[]{:S(2)}) async-start(bf16[128,64,4,16]{0,2,3,1:T(4,128)(2,1)} %copy.1028), calls=%async_computation.41 | async-start | bytes 2097152 | tf_op jit(solution)/shard_map/all_to_all | solution.py:37
  2197.1 31.0 %all-to-all-start.42 = ((bf16[128,8,4,128]{0,2,1,3:T(4,128)(2,1)}), bf16[128,8,4,128]{0,2,1,3:T(4,128)(2,1)}, u32[]{:S(2)}, u32[]{:S(2)}) async-start(bf16[128,8,4,128]{0,2,1,3:T(4,128)(2,1)} %copy.1035), calls=%async_computation.42 | async-start | bytes 2097152 | tf_op jit(solution)/shard_map/all_to_all | solution.py:33
  2237.5 52.4 %all-to-all-start.43 = ((bf16[128,64,4,16]{0,2,3,1:T(4,128)(2,1)}), bf16[128,64,4,16]{0,2,3,1:T(4,128)(2,1)S(1)}, u32[]{:S(2)}, u32[]{:S(2)}) async-start(bf16[128,64,4,16]{0,2,3,1:T(4,128)(2,1)} %copy.1040), calls=%async_computation.43 | async-start | bytes 2097152 | tf_op jit(solution)/shard_map/all_to_all | solution.py:37
  (271 other events, 1206.1 us)
where the time goes:
time: 2350 us; the launch traced here: 2330 us
  waiting for transfers between devices  720 us (31%)
  blocking collectives  446 us (19%)
  local copies, waits for them, and re-layouts  415 us (18%)
  matrix products  333 us (14%)
  starting transfers between devices  245 us (10%)
  other arithmetic  166 us (7%)
    all_to_all x21, waiting for transfers between devices, to_features(): lax.all_to_all(values, 'tensor', split_axis=1, concat_axis=3, tiled=True)  350 us
    psum x22, blocking collectives, row_total(): return lax.psum(values, 'tensor')  326 us
    all_to_all x19, waiting for transfers between devices, to_hidden(): lax.all_to_all(values, 'tensor', split_axis=3, concat_axis=1, tiled=True)  288 us
    dynamic_update_slice x63, other arithmetic, store_at(): lax.dynamic_update_index_in_dim(stored, jnp.where(is_valid, member, forme...  136 us
    all_to_all x21, starting transfers between devices, to_features(): lax.all_to_all(values, 'tensor', split_axis=1, concat_axis=3, tiled=True)  92.3 us
    all_to_all x3, blocking collectives, to_hidden(): lax.all_to_all(values, 'tensor', split_axis=3, concat_axis=1, tiled=True)  91.3 us
    dynamic_slice x47, local copies, waits for them, and re-layouts, store_at(): former = lax.dynamic_index_in_dim(stored, micro_slot, 0, keepdims=False)  87.4 us
    all_to_all x19, starting transfers between devices, to_hidden(): lax.all_to_all(values, 'tensor', split_axis=3, concat_axis=1, tiled=True)  83.1 us
  transfers between devices with their start and end apart: 60, of which 56 were waited for; matrix products, arithmetic and copies ran while one was open for 21% of the time, Pallas kernels for 0%

commit v1 on v0

v1 whole, which is shorter than its diff:
```python
import math

import jax
import jax.numpy as jnp
from jax import lax
from jax.sharding import PartitionSpec as P

EPS = 1e-05
TANH_SCALE = math.sqrt(2.0 / math.pi)
CUBIC_COEF = 0.044715
F32 = jnp.float32
BF16 = jnp.bfloat16


def gelu_value(preact):
    tanh_val = jnp.tanh(TANH_SCALE * (preact + CUBIC_COEF * preact * preact * preact))
    return 0.5 * preact * (1.0 + tanh_val)


def gelu_slope(preact):
    tanh_val = jnp.tanh(TANH_SCALE * (preact + CUBIC_COEF * preact * preact * preact))
    return 0.5 * (1.0 + tanh_val) + 0.5 * preact * (
        1.0 - tanh_val * tanh_val
    ) * TANH_SCALE * (1.0 + 3.0 * CUBIC_COEF * preact * preact)


def dot(spec, left, right):
    return jnp.einsum(spec, left, right, preferred_element_type=F32)


def swap(values, axis):
    return lax.all_to_all(values, axis, split_axis=0, concat_axis=0, tiled=True)


def body(inputs, cotangent, norm_gain, first_factor, second_factor, third_factor, fourth_factor):
    sections = lax.axis_size("pipe")
    group = lax.axis_index("pipe")
    ranks = lax.axis_size("tensor")
    rank = lax.axis_index("tensor")
    micro_count, tokens, width_dev = inputs.shape
    width = width_dev * ranks
    share = micro_count // sections
    span = share * tokens
    blocks, block_size = first_factor.shape[1], first_factor.shape[2]
    expand = first_factor.shape[3] // block_size
    cols, mix_width = second_factor.shape[1], second_factor.shape[2]
    all_blocks = mix_width // expand
    inner = expand * cols

    def whole_stream(values):
        mine = lax.dynamic_slice_in_dim(values, group * share, share, 0)
        mine = mine.reshape(span, width_dev).T
        return lax.all_gather(mine, "tensor", axis=0, tiled=True)

    def to_cols(values):
        return (
            values.reshape(all_blocks, expand, cols, span)
            .transpose(2, 0, 1, 3)
            .reshape(cols, mix_width, span)
        )

    def to_blocks(values):
        return (
            values.reshape(cols, all_blocks, expand, span)
            .transpose(1, 2, 0, 3)
            .reshape(all_blocks, inner, span)
        )

    def over_pipe(values):
        return lax.all_gather(values, "pipe", axis=0, tiled=False)

    stream = whole_stream(inputs)
    grad = whole_stream(cotangent)
    gains = over_pipe(lax.all_gather(norm_gain[0], "tensor", axis=0, tiled=True))
    first = first_factor[0].reshape(blocks, block_size, expand, ranks, cols)
    first = first.transpose(3, 0, 2, 4, 1).reshape(ranks * blocks, inner, block_size)
    first = over_pipe(swap(first, "tensor"))
    second = over_pipe(second_factor[0])
    third = over_pipe(third_factor[0])
    fourth = fourth_factor[0].reshape(blocks, expand, ranks, cols, block_size)
    fourth = fourth.transpose(2, 0, 1, 3, 4).reshape(ranks * blocks, inner, block_size)
    fourth = over_pipe(swap(fourth, "tensor"))

    records = []
    outs = []
    for layer in range(sections):
        f = stream.astype(F32)
        inv = lax.rsqrt(jnp.mean(f * f, axis=0) + EPS)
        normed = (f * inv * gains[layer][:, None]).astype(BF16)
        normed = normed.reshape(all_blocks, block_size, span)
        spread = to_cols(dot("ikj,ijt->ikt", first[layer], normed).astype(BF16))
        preact = dot("cme,cmt->cet", second[layer], spread)
        act = gelu_value(preact).astype(BF16)
        mixed = to_blocks(dot("cem,cet->cmt", third[layer], act).astype(BF16))
        branch = dot("ikj,ikt->ijt", fourth[layer], mixed).astype(BF16)
        branch = lax.psum(branch.reshape(width, span), "tensor")
        records.append((stream, inv, normed, spread, preact, act, mixed))
        stream = (f + branch.astype(F32)).astype(BF16)
        outs.append(lax.dynamic_slice_in_dim(stream, rank * width_dev, width_dev, 0))

    def placed(members):
        moved = swap(jnp.stack(members), "pipe")
        moved = moved.reshape(sections, width_dev, share, tokens)
        return moved.transpose(0, 2, 3, 1).reshape(1, micro_count, tokens, width_dev)

    section_out = placed(outs)

    grads = [None] * sections
    parts = [None] * sections
    for layer in reversed(range(sections)):
        stream, inv, normed, spread, preact, act, mixed = records[layer]
        gain = gains[layer][:, None]
        grad_blocks = grad.reshape(all_blocks, block_size, span)
        part_four = dot("ikt,ijt->ikj", mixed, grad_blocks)
        grad_mixed = to_cols(dot("ikj,ijt->ikt", fourth[layer], grad_blocks).astype(BF16))
        part_three = dot("cet,cmt->cem", act, grad_mixed)
        grad_act = dot("cem,cmt->cet", third[layer], grad_mixed)
        grad_pre = (grad_act * gelu_slope(preact)).astype(BF16)
        part_two = dot("cmt,cet->cme", spread, grad_pre)
        grad_spread = to_blocks(dot("cme,cet->cmt", second[layer], grad_pre).astype(BF16))
        part_one = dot("ikt,ijt->ikj", grad_spread, normed)
        grad_norm = dot("ikj,ikt->ijt", first[layer], grad_spread).astype(BF16)
        grad_norm = lax.psum(grad_norm.reshape(width, span), "tensor").astype(F32)
        f = stream.astype(F32)
        my_norm = lax.dynamic_slice_in_dim(grad_norm, rank * width_dev, width_dev, 0)
        my_f = lax.dynamic_slice_in_dim(stream, rank * width_dev, width_dev, 0).astype(F32)
        part_gain = jnp.sum(my_norm * my_f * inv, axis=1)
        scaled = grad_norm * gain
        inner_sum = jnp.sum(scaled * f, axis=0)
        grad = (
            grad.astype(F32) + scaled * inv - f * (inv * inv * inv * inner_sum / width)
        ).astype(BF16)
        grads[layer] = lax.dynamic_slice_in_dim(grad, rank * width_dev, width_dev, 0)
        parts[layer] = (
            part_gain,
            part_one.astype(BF16),
            part_two.astype(BF16),
            part_three.astype(BF16),
            part_four.astype(BF16),
        )

    section_grad = placed(grads)

    def collected(which):
        moved = swap(jnp.stack([part[which] for part in parts]), "pipe")
        return jnp.sum(moved.astype(F32), axis=0)

    def at_home(values):
        values = swap(values.astype(BF16), "tensor")
        return values.reshape(ranks, blocks, expand, cols, block_size).astype(F32)

    gain_grad = collected(0)
    first_grad = at_home(collected(1)).transpose(1, 4, 2, 0, 3)
    fourth_grad = at_home(collected(4)).transpose(1, 2, 0, 3, 4)
    return (
        section_out,
        section_grad,
        gain_grad[None],
        first_grad.reshape(1, blocks, block_size, expand * block_size),
        collected(2)[None],
        collected(3)[None],
        fourth_grad.reshape(1, blocks, expand * block_size, block_size),
    )


def solution(mesh):
    factor = P("pipe", "tensor", None, None)
    stream = P(None, None, "tensor")
    result = P("pipe", None, None, "tensor")
    return jax.shard_map(
        body,
        mesh=mesh,
        in_specs=(stream, stream, P("pipe", "tensor"), factor, factor, factor, factor),
        out_specs=(result, result, P("pipe", "tensor"), factor, factor, factor, factor),
        check_vma=False,
    )
```

time: 2350 us -> 1840 us (0.78)
  waiting for transfers between devices: 720 us -> 1070 us
  blocking collectives: 446 us -> 111 us
  starting transfers between devices: 245 us -> 42.8 us
  local copies, waits for them, and re-layouts: 415 us -> 246 us
  matrix products: 333 us -> 192 us
    psum x0 -> x7, waiting for transfers between devices: none -> 666 us  [the longest x4 412 us: body(): branch = lax.psum(branch.reshape(width, span), 'tensor')]
    all_to_all x40 -> x9, waiting for transfers between devices: 638 us -> 194 us  [swap(): return lax.all_to_all(values, axis, split_axis=0, concat_axis=0, tiled=True)]
    psum x22 -> x0, blocking collectives: 326 us -> none  [row_total(): return lax.psum(values, 'tensor')]
    all_gather x0 -> x6, waiting for transfers between devices: none -> 211 us  [the longest x4 210 us: over_pipe(): return lax.all_gather(values, 'pipe', axis=0, tiled=False)]
    dynamic_update_slice x63 -> x0, other arithmetic: 136 us -> none  [store_at(): lax.dynamic_update_index_in_dim(stored, jnp.where(is_valid, member, forme...]
    all_to_all x40 -> x9, starting transfers between devices: 175 us -> 41 us  [swap(): return lax.all_to_all(values, axis, split_axis=0, concat_axis=0, tiled=True)]
    reshape x0 -> x27, local copies, waits for them, and re-layouts: none -> 133 us  [the longest x8 29.9 us: to_blocks(): values.reshape(cols, all_blocks, expand, span).transpose(1, 2, 0, 3)]
    dot_general x121 -> x48, matrix products: 313 us -> 192 us  [dot(): return jnp.einsum(spec, left, right, preferred_element_type=F32)]
  transfers between devices with their start and end apart: 60 -> 22, of which waited for: 56 -> 16; matrix products, arithmetic and copies ran while one was open for 21% -> 17% of each run, Pallas kernels for 0% -> 0%
where the time goes in v1:
time: 1840 us; the launch traced here: 1820 us
  waiting for transfers between devices  1070 us (58%)
  local copies, waits for them, and re-layouts  246 us (13%)
  matrix products  192 us (10%)
  other arithmetic  143 us (8%)
  blocking collectives  111 us (6%)
  starting transfers between devices  42.8 us (2%)
    psum x4, waiting for transfers between devices, body(): branch = lax.psum(branch.reshape(width, span), 'tensor')  412 us
    psum x3, waiting for transfers between devices, body(): grad_norm = lax.psum(grad_norm.reshape(width, span), 'tensor').astype(F32)  254 us
    all_gather x4, waiting for transfers between devices, over_pipe(): return lax.all_gather(values, 'pipe', axis=0, tiled=False)  210 us
    all_to_all x9, waiting for transfers between devices, swap(): return lax.all_to_all(values, axis, split_axis=0, concat_axis=0, tiled=True)  194 us
    dot_general x48, matrix products, dot(): return jnp.einsum(spec, left, right, preferred_element_type=F32)  192 us
    all_to_all x2, blocking collectives, swap(): return lax.all_to_all(values, axis, split_axis=0, concat_axis=0, tiled=True)  88 us
    unnamed x170, local copies, waits for them, and re-layouts  43.1 us
    all_to_all x9, starting transfers between devices, swap(): return lax.all_to_all(values, axis, split_axis=0, concat_axis=0, tiled=True)  41 us
  transfers between devices with their start and end apart: 22, of which 16 were waited for; matrix products, arithmetic and copies ran while one was open for 17% of the time, Pallas kernels for 0%

profile of v1, /device:TPU:0, one launch (start us, length us, event | category | flops | bytes accessed | tf_op | source)
XLA Modules:
  0.0 1822.0 jit_solution(6714251652788538811)
XLA Ops:
  11.6 58.3 %all_to_all.59 = bf16[64,64,128]{2,1,0:T(8,128)(2,1)} all-to-all(bf16[64,64,128]{2,1,0:T(8,128)(2,1)S(1)} %bitcast.407), channel_id=1, replica_groups=mesh['pipe'=4,'tensor'=8] {'tensor'}, dimensions={0} | all-to-all | bytes 2097152 | tf_op jit(solution)/shard_map/all_to_all | solution.py:32
  71.6 29.7 %all_to_all.60 = bf16[64,64,128]{2,1,0:T(8,128)(2,1)} all-to-all(bf16[64,64,128]{2,1,0:T(8,128)(2,1)S(1)} %bitcast.409), channel_id=1, replica_groups=mesh['pipe'=4,'tensor'=8] {'tensor'}, dimensions={0} | all-to-all | bytes 2097152 | tf_op jit(solution)/shard_map/all_to_all | solution.py:32
  101.4 14.0 all-gather
  115.4 9.5 all-gather.4
  131.6 6.4 copy.453
  141.2 82.6 %all-gather.14.cloned.1.call-done = bf16[4,16,256,256]{3,2,1,0:T(8,128)(2,1)} async-done(((bf16[1,16,256,256]{3,2,1,0:T(8,128)(2,1)}), bf16[4,16,256,256]{3,2,1,0:T(8,128)(2,1)}) %all-gather.14.cloned.1.call-update) | async-done | bytes 8388624 | tf_op jit(solution)/shard_map/all_gather | solution.py:70
  228.9 84.2 %all-gather.16.cloned.1.call-done = bf16[4,16,256,256]{3,2,1,0:T(8,128)(2,1)} async-done(((bf16[1,16,256,256]{3,2,1,0:T(8,128)(2,1)}), bf16[4,16,256,256]{3,2,1,0:T(8,128)(2,1)}) %all-gather.16.cloned.1.call-update) | async-done | bytes 8388624 | tf_op jit(solution)/shard_map/all_gather | solution.py:70
  323.9 43.6 %all-gather.22.cloned.1.call-done = bf16[256,64,128]{2,1,0:T(8,128)(2,1)} async-done(((bf16[64,64,128]{2,1,0:T(8,128)(2,1)}), bf16[256,64,128]{2,1,0:T(8,128)(2,1)}) %all-gather.22.cloned.1.call-update) | async-done | bytes 4194320 | tf_op jit(solution)/shard_map/all_gather | solution.py:70
  372.2 6.3 copy.323
  378.8 96.4 %all-reduce.9.cloned.1.call-done = bf16[8192,256]{0,1:T(8,128)(2,1)} async-done(((bf16[8192,256]{0,1:T(8,128)(2,1)}), bf16[8192,256]{0,1:T(8,128)(2,1)}) %all-reduce.9.cloned.1.call-update) | async-done | bytes 4194320 | tf_op jit(solution)/shard_map/psum | solution.py:96
  485.9 6.4 copy.454
  518.6 6.3 copy.331
  527.4 94.3 %all-reduce.11.cloned.1.call-done = bf16[8192,256]{0,1:T(8,128)(2,1)} async-done(((bf16[8192,256]{0,1:T(8,128)(2,1)}), bf16[8192,256]{0,1:T(8,128)(2,1)}) %all-reduce.11.cloned.1.call-update) | async-done | bytes 4194320 | tf_op jit(solution)/shard_map/psum | solution.py:96
  632.3 6.4 copy.455
  667.2 6.4 copy.339
  673.8 6.4 copy.350
  684.7 85.6 %all-reduce.13.cloned.1.call-done = bf16[8192,256]{0,1:T(8,128)(2,1)} async-done(((bf16[8192,256]{0,1:T(8,128)(2,1)}), bf16[8192,256]{0,1:T(8,128)(2,1)}) %all-reduce.13.cloned.1.call-update) | async-done | bytes 4194320 | tf_op jit(solution)/shard_map/psum | solution.py:96
  781.0 6.4 copy.456
  794.6 6.9 fusion.26
  820.2 6.3 copy.356
  826.6 96.7 %all-reduce.15.cloned.1.call-done = bf16[8192,256]{0,1:T(8,128)(2,1)} async-done(((bf16[8192,256]{0,1:T(8,128)(2,1)}), bf16[8192,256]{0,1:T(8,128)(2,1)}) %all-reduce.15.cloned.1.call-update) | async-done | bytes 4194320 | tf_op jit(solution)/shard_map/psum | solution.py:123
  929.2 6.5 subtract_convert_fusion
  935.6 6.4 copy.457
  970.3 6.4 copy.363
  976.7 96.7 %all-reduce.17.cloned.1.call-done = bf16[8192,256]{0,1:T(8,128)(2,1)} async-done(((bf16[8192,256]{0,1:T(8,128)(2,1)}), bf16[8192,256]{0,1:T(8,128)(2,1)}) %all-reduce.17.cloned.1.call-update) | async-done | bytes 4194320 | tf_op jit(solution)/shard_map/psum | solution.py:123
  1079.3 6.3 fusion.13
  1085.6 6.4 copy.458
  1120.3 6.4 copy.370
  1126.7 6.1 convert_bitcast_fusion.14
  1146.8 6.4 copy.347
  1163.1 60.3 %all-reduce.19.cloned.1.call-done = bf16[8192,256]{0,1:T(8,128)(2,1)} async-done(((bf16[8192,256]{0,1:T(8,128)(2,1)}), bf16[8192,256]{0,1:T(8,128)(2,1)}) %all-reduce.19.cloned.1.call-update) | async-done | bytes 4194320 | tf_op jit(solution)/shard_map/psum | solution.py:123
  1229.4 6.2 fusion.6
  1235.5 6.5 copy.459
  1257.4 5.8 fusion.41
  1280.7 6.3 copy.377
  1307.8 6.7 convert_element_type.334
  1327.9 135.8 %all-reduce.21.cloned.1.call-done = (bf16[8192,256]{0,1:T(8,128)(2,1)}, bf16[8192,256]{0,1:T(8,128)(2,1)}) async-done(((bf16[8192,256]{0,1:T(8,128)(2,1)}, bf16[8192,256]{0,1:T(8,128)(2,1)}), (bf16[8192,256]{0,1:T(8,128)(2,1)}, bf16[8192,256]{0,1:T(8,128)(2,1)})) %all-reduce.21.cloned.1.call-update) | async-done | bytes 8388624 | tf_op jit(solution)/shard_map/psum | solution.py:96
  1495.5 22.2 %all-to-all-done.10 = bf16[64,64,128]{2,1,0:T(8,128)(2,1)S(1)} async-done(((bf16[64,64,128]{2,1,0:T(8,128)(2,1)}), bf16[64,64,128]{2,1,0:T(8,128)(2,1)S(1)}, u32[]{:S(2)}, u32[]{:S(2)}) %all-to-all-start.10) | async-done | bytes 1048608 | tf_op jit(solution)/shard_map/all_to_all | solution.py:32
  1532.6 15.2 all-to-all-done.6
  1552.8 6.7 convert_bitcast_fusion.2
  1569.5 6.5 convert_bitcast_fusion.4
  1597.1 15.4 all-to-all-done.3
  1612.5 5.9 all-to-all-start.8
  1631.1 79.0 %all-to-all-done.8 = bf16[4,16,256,256]{3,2,1,0:T(8,128)(2,1)} async-done(((bf16[4,16,256,256]{3,2,1,0:T(8,128)(2,1)}), bf16[4,16,256,256]{3,2,1,0:T(8,128)(2,1)}, u32[]{:S(2)}, u32[]{:S(2)}) %all-to-all-start.8) | async-done | bytes 8388640 | tf_op jit(solution)/shard_map/all_to_all | solution.py:32
  1726.2 6.1 copy.349
  1738.7 7.5 convert_reduce_fusion
  1746.2 61.4 %all-to-all-done.7 = bf16[4,16,256,256]{3,2,1,0:T(8,128)(2,1)} async-done(((bf16[4,16,256,256]{3,2,1,0:T(8,128)(2,1)}), bf16[4,16,256,256]{3,2,1,0:T(8,128)(2,1)}, u32[]{:S(2)}, u32[]{:S(2)}) %all-to-all-start.7) | async-done | bytes 8388640 | tf_op jit(solution)/shard_map/all_to_all | solution.py:32
  1807.6 7.4 convert_reduce_fusion.1
  (333 shorter events, 439.1 us)
Async XLA Ops:
  7.2 117.7 %all-gather.12.cloned.1.call-start = ((), (), s32[]{:S(2)}) async-start(), calls=%async_computation.11 | async-start | bytes 4718592 | tf_op jit(solution)/shard_map/all_gather | solution.py:53
  9.6 128.3 %all-gather.20.cloned.1.call-start = ((), (), s32[]{:S(2)}) async-start(), calls=%async_computation.21 | async-start | bytes 5242880 | tf_op jit(solution)/shard_map/all_gather | solution.py:70
  11.6 59.7 %copy-start.70 = (bf16[1,8,512,128]{3,2,1,0:T(8,128)(2,1)S(1)}, bf16[1,8,512,128]{3,2,1,0:T(8,128)(2,1)}, u32[]{:S(2)}) copy-start(bf16[1,8,512,128]{3,2,1,0:T(8,128)(2,1)} %param.13) | copy-start | bytes 3145732
  69.9 153.9 %all-gather.14.cloned.1.call-start = ((), (), s32[]{:S(2)}) async-start(), calls=%async_computation.12 | async-start | bytes 10485760 | tf_op jit(solution)/shard_map/all_gather | solution.py:70
  70.6 30.7 %copy-start.83 = (f32[1,1024]{1,0:T(1,128)S(1)}, f32[1,1024]{1,0:T(1,128)}, u32[]{:S(2)}) copy-start(f32[1,1024]{1,0:T(1,128)} %param.9) | copy-start | bytes 12292
  70.7 242.5 %all-gather.16.cloned.1.call-start = ((), (), s32[]{:S(2)}) async-start(), calls=%async_computation.13 | async-start | bytes 10485760 | tf_op jit(solution)/shard_map/all_gather | solution.py:70
  71.2 296.3 %all-gather.22.cloned.1.call-start = ((), (), s32[]{:S(2)}) async-start(), calls=%async_computation.22 | async-start | bytes 5242880 | tf_op jit(solution)/shard_map/all_gather | solution.py:70
  101.3 373.9 %all-reduce.9.cloned.1.call-start = ((), (), s32[]{:S(2)}) async-start(), calls=%async_computation.14 | async-start | bytes 8388608 | tf_op jit(solution)/shard_map/psum | solution.py:96
  124.9 6.7 copy-start.73
  124.9 355.8 %copy-start.71 = (f32[1,1,8192]{2,1,0:T(1,128)}, f32[1,1,8192]{2,1,0:T(1,128)S(1)}, u32[]{:S(2)}) copy-start(f32[1,1,8192]{2,1,0:T(1,128)S(1)} %get-tuple-element.47) | copy-start | bytes 98308
  141.2 87.8 %copy-start.35 = (bf16[64,256,64]{1,2,0:T(8,128)(2,1)}, bf16[64,256,64]{1,2,0:T(8,128)(2,1)S(1)}, u32[]{:S(2)}) copy-start(bf16[64,256,64]{1,2,0:T(8,128)(2,1)S(1)} %convolution_convert_fusion.15) | copy-start | bytes 6291460
  323.9 54.6 %copy-start.22 = (bf16[64,4,16,256]{3,2,1,0:T(8,128)(2,1)}, bf16[64,4,16,256]{3,2,1,0:T(8,128)(2,1)S(1)}, u32[]{:S(2)}) copy-start(bf16[64,4,16,256]{3,2,1,0:T(8,128)(2,1)S(1)} %copy.321) | copy-start | bytes 6291460
  378.5 243.2 %all-reduce.11.cloned.1.call-start = ((), (), s32[]{:S(2)}) async-start(), calls=%async_computation.15 | async-start | bytes 8388608 | tf_op jit(solution)/shard_map/psum | solution.py:96
  525.0 148.8 %all-gather.18.cloned.1.call-start = ((), (), s32[]{:S(2)}) async-start(), calls=%async_computation.17 | async-start | bytes 4718592 | tf_op jit(solution)/shard_map/all_gather | solution.py:53
  526.9 243.4 %all-reduce.13.cloned.1.call-start = ((), (), s32[]{:S(2)}) async-start(), calls=%async_computation.16 | async-start | bytes 8388608 | tf_op jit(solution)/shard_map/psum | solution.py:96
  673.5 249.7 %all-reduce.15.cloned.1.call-start = ((), (), s32[]{:S(2)}) async-start(), calls=%async_computation.18 | async-start | bytes 8388608 | tf_op jit(solution)/shard_map/psum | solution.py:123
  794.6 7.0 copy-start.59
  826.5 246.8 %all-reduce.17.cloned.1.call-start = ((), (), s32[]{:S(2)}) async-start(), calls=%async_computation.19 | async-start | bytes 8388608 | tf_op jit(solution)/shard_map/psum | solution.py:123
  923.3 5.9 copy-start.13
  945.4 6.2 copy-start.63
  976.7 246.8 %all-reduce.19.cloned.1.call-start = ((), (), s32[]{:S(2)}) async-start(), calls=%async_computation.20 | async-start | bytes 8388608 | tf_op jit(solution)/shard_map/psum | solution.py:123
  1073.4 5.9 copy-start.11
  1095.3 6.2 copy-start.65
  1160.6 62.9 %copy-start.72 = (f32[1,1,8192]{2,1,0:T(1,128)S(1)}, f32[1,1,8192]{2,1,0:T(1,128)}, u32[]{:S(2)}) copy-start(f32[1,1,8192]{2,1,0:T(1,128)} %copy-done.71) | copy-start | bytes 98308
  1163.1 65.4 %copy-start.80 = (f32[256]{0:T(256)S(1)}, f32[256]{0:T(256)}, u32[]{:S(2)}) copy-start(f32[256]{0:T(256)} %copy-done.79) | copy-start | bytes 3076
  1163.1 65.4 %copy-start.76 = (f32[256]{0:T(256)S(1)}, f32[256]{0:T(256)}, u32[]{:S(2)}) copy-start(f32[256]{0:T(256)} %copy-done.75) | copy-start | bytes 3076
  1223.5 5.9 copy-start.12
  1235.5 6.5 copy-start.23
  1248.3 54.4 %all-to-all-start.9 = ((bf16[4,64,64,128]{3,2,1,0:T(8,128)(2,1)}), bf16[4,64,64,128]{3,2,1,0:T(8,128)(2,1)}, u32[]{:S(2)}, u32[]{:S(2)}) async-start(bf16[4,64,64,128]{3,2,1,0:T(8,128)(2,1)} %pad_maximum_fusion.3), calls=%async_computation.9 | async-start | bytes 8388608 | tf_op jit(solution)/shard_map/all_to_all | solution.py:32
  1253.2 210.5 %all-reduce.21.cloned.1.call-start = ((), (), s32[]{:S(2)}) async-start(), calls=%async_computation.23 | async-start | bytes 16777216 | tf_op jit(solution)/shard_map/psum | solution.py:96
  1257.0 6.2 copy-start.66
  1263.2 8.4 copy-start.48
  1275.4 11.6 copy-start.32
  1302.7 176.2 %all-to-all-start.5 = ((bf16[4,64,64,128]{3,2,1,0:T(8,128)(2,1)}), bf16[4,64,64,128]{3,2,1,0:T(8,128)(2,1)}, u32[]{:S(2)}, u32[]{:S(2)}) async-start(bf16[4,64,64,128]{3,2,1,0:T(8,128)(2,1)} %pad_maximum_fusion.2), calls=%async_computation.5 | async-start | bytes 8388608 | tf_op jit(solution)/shard_map/all_to_all | solution.py:32
  1307.8 6.7 copy-start.8
  1468.4 7.0 copy-start.82
  1478.9 8.4 all-to-all-start.4
  1487.3 30.4 %all-to-all-start.10 = ((bf16[64,64,128]{2,1,0:T(8,128)(2,1)}), bf16[64,64,128]{2,1,0:T(8,128)(2,1)S(1)}, u32[]{:S(2)}, u32[]{:S(2)}) async-start(bf16[64,64,128]{2,1,0:T(8,128)(2,1)} %reduce_sum.175), calls=%async_computation.10 | async-start | bytes 2097152 | tf_op jit(solution)/shard_map/all_to_all | solution.py:32
  1517.7 30.1 %all-to-all-start.6 = ((bf16[64,64,128]{2,1,0:T(8,128)(2,1)}), bf16[64,64,128]{2,1,0:T(8,128)(2,1)S(1)}, u32[]{:S(2)}, u32[]{:S(2)}) async-start(bf16[64,64,128]{2,1,0:T(8,128)(2,1)} %reduce_sum.172), calls=%async_computation.6 | async-start | bytes 2097152 | tf_op jit(solution)/shard_map/all_to_all | solution.py:32
  1548.7 34.6 %all-to-all-start.2 = ((bf16[4,1024,256]{2,1,0:T(8,128)(2,1)}), bf16[4,1024,256]{2,1,0:T(8,128)(2,1)S(1)}, u32[]{:S(2)}, u32[]{:S(2)}) async-start(bf16[4,1024,256]{2,1,0:T(8,128)(2,1)} %pad_maximum_fusion.4), calls=%async_computation.2 | async-start | bytes 4194304 | tf_op jit(solution)/shard_map/all_to_all | solution.py:32
  1552.8 6.7 copy-start.58
  1552.8 6.7 copy-start.64
  1583.3 9.9 copy-start.50
  1583.3 29.3 %all-to-all-start.3 = ((bf16[4,1024,256]{2,1,0:T(8,128)(2,1)}), bf16[4,1024,256]{2,1,0:T(8,128)(2,1)}, u32[]{:S(2)}, u32[]{:S(2)}) async-start(bf16[4,1024,256]{2,1,0:T(8,128)(2,1)} %pad_maximum_fusion.5), calls=%async_computation.3 | async-start | bytes 4194304 | tf_op jit(solution)/shard_map/all_to_all | solution.py:32
  1587.8 5.4 copy-start.67
  1612.5 97.6 %all-to-all-start.8 = ((bf16[4,16,256,256]{3,2,1,0:T(8,128)(2,1)}), bf16[4,16,256,256]{3,2,1,0:T(8,128)(2,1)}, u32[]{:S(2)}, u32[]{:S(2)}) async-start(bf16[4,16,256,256]{3,2,1,0:T(8,128)(2,1)} %pad_maximum_fusion.1), calls=%async_computation.8 | async-start | bytes 16777216 | tf_op jit(solution)/shard_map/all_to_all | solution.py:32
  1710.2 97.5 %all-to-all-start.7 = ((bf16[4,16,256,256]{3,2,1,0:T(8,128)(2,1)}), bf16[4,16,256,256]{3,2,1,0:T(8,128)(2,1)}, u32[]{:S(2)}, u32[]{:S(2)}) async-start(bf16[4,16,256,256]{3,2,1,0:T(8,128)(2,1)} %pad_maximum_fusion), calls=%async_computation.7 | async-start | bytes 16777216 | tf_op jit(solution)/shard_map/all_to_all | solution.py:32
  1738.7 76.3 %copy-start.1 = (bf16[8,128,1024]{2,1,0:T(8,128)(2,1)S(1)}, bf16[8,128,1024]{2,1,0:T(8,128)(2,1)}, u32[]{:S(2)}) copy-start(bf16[8,128,1024]{2,1,0:T(8,128)(2,1)} %param.7) | copy-start | bytes 6291460
  (58 other events, 177.6 us)
Sparse Core Ops, SparseCore 0:
  10.2 69.5 all-gather.11
  81.6 52.6 all-gather.19
  136.1 87.5 all-gather.13
  225.5 87.6 all-gather.15
  314.8 52.6 all-gather.21
  378.7 96.5 all-reduce.8
  525.1 96.5 all-reduce.10
  623.9 47.1 all-gather.17
  673.7 96.6 all-reduce.12
  826.7 96.5 all-reduce.14
  976.8 96.5 all-reduce.16
  1126.8 96.5 all-reduce.18
  1287.2 176.4 all-reduce.20

commit v2 on v1

v2 whole, which is shorter than its diff:
```python
import math

import jax
import jax.numpy as jnp
from jax import lax
from jax.experimental.layout import Layout, with_layout_constraint
from jax.sharding import PartitionSpec as P

EPS = 1e-05
TANH_SCALE = math.sqrt(2.0 / math.pi)
CUBIC_COEF = 0.044715
F32 = jnp.float32
BF16 = jnp.bfloat16


def gelu_value(preact):
    tanh_val = jnp.tanh(TANH_SCALE * (preact + CUBIC_COEF * preact * preact * preact))
    return 0.5 * preact * (1.0 + tanh_val)


def gelu_slope(preact):
    tanh_val = jnp.tanh(TANH_SCALE * (preact + CUBIC_COEF * preact * preact * preact))
    return 0.5 * (1.0 + tanh_val) + 0.5 * preact * (
        1.0 - tanh_val * tanh_val
    ) * TANH_SCALE * (1.0 + 3.0 * CUBIC_COEF * preact * preact)


def dot(spec, left, right):
    return jnp.einsum(spec, left, right, preferred_element_type=F32)


def swap(values, axis):
    return lax.all_to_all(values, axis, split_axis=0, concat_axis=0, tiled=True)


def body(inputs, cotangent, norm_gain, first_factor, second_factor, third_factor, fourth_factor):
    sections = lax.axis_size("pipe")
    group = lax.axis_index("pipe")
    ranks = lax.axis_size("tensor")
    rank = lax.axis_index("tensor")
    micro_count, tokens, width_dev = inputs.shape
    width = width_dev * ranks
    share = micro_count // sections
    blocks, block_size = first_factor.shape[1], first_factor.shape[2]
    expand = first_factor.shape[3] // block_size
    cols, mix_width = second_factor.shape[1], second_factor.shape[2]
    all_blocks = mix_width // expand
    inner = expand * cols

    def rows_first(values):
        return with_layout_constraint(values, Layout(major_to_minor=(0, 1)))

    def whole_stream(values):
        mine = lax.dynamic_slice_in_dim(values, group * share, share, 0)
        mine = mine.reshape(share * tokens, width_dev).T
        full = rows_first(lax.all_gather(rows_first(mine), "tensor", axis=0, tiled=True))
        return [full[:, k * tokens : (k + 1) * tokens] for k in range(share)]

    def to_cols(values):
        return (
            values.reshape(all_blocks, expand, cols, tokens)
            .transpose(2, 0, 1, 3)
            .reshape(cols, mix_width, tokens)
        )

    def to_blocks(values):
        return (
            values.reshape(cols, all_blocks, expand, tokens)
            .transpose(1, 2, 0, 3)
            .reshape(all_blocks, inner, tokens)
        )

    def my_rows(values):
        return lax.dynamic_slice_in_dim(values, rank * width_dev, width_dev, 0)

    waiting = [None] * share
    newest = [None]

    def start_sum(k, partial, scatter):
        if newest[0] is not None:
            last = newest[0]
            partial, waiting[last] = lax.optimization_barrier((partial, waiting[last]))
        if scatter:
            waiting[k] = lax.psum_scatter(partial, "tensor", scatter_dimension=0, tiled=True)
        else:
            waiting[k] = rows_first(lax.psum(partial, "tensor"))
        newest[0] = k

    def quarters(values):
        moved = swap(values, "pipe")
        return moved.reshape((sections, moved.shape[0] // sections) + moved.shape[1:])

    def from_quarter(values):
        return swap(jnp.tile(values, (sections,) + (1,) * (values.ndim - 1)), "pipe")

    first = first_factor[0].reshape(blocks, block_size, expand, ranks, cols)
    first = first.transpose(3, 0, 2, 4, 1).reshape(ranks, blocks, inner, block_size)
    fourth = fourth_factor[0].reshape(blocks, expand, ranks, cols, block_size)
    fourth = fourth.transpose(2, 0, 1, 3, 4).reshape(ranks, blocks, inner, block_size)
    outer = quarters(swap(jnp.stack([first, fourth], axis=1), "tensor"))
    second = quarters(second_factor[0])
    third = quarters(third_factor[0])
    weights = []
    for layer in range(sections):
        own = (outer[layer], second[layer], third[layer])
        if weights:
            own, weights[-1] = lax.optimization_barrier((own, weights[-1]))
        weights.append(tuple(from_quarter(member) for member in own))
    outer_shape = (all_blocks, inner, block_size)
    factors = [
        (w[0][:, 0].reshape(outer_shape), w[1], w[2], w[0][:, 1].reshape(outer_shape))
        for w in weights
    ]

    streams = whole_stream(inputs)
    grads = whole_stream(cotangent)
    gains = lax.all_gather(norm_gain[0], "tensor", axis=0, tiled=True)
    gains = lax.all_gather(gains, "pipe", axis=0, tiled=False)

    def forward(layer, stream):
        first, second, third, fourth = factors[layer]
        f = stream.astype(F32)
        inv = lax.rsqrt(jnp.mean(f * f, axis=0) + EPS)
        normed = (f * inv * gains[layer][:, None]).astype(BF16)
        normed = normed.reshape(all_blocks, block_size, tokens)
        spread = to_cols(dot("ikj,ijt->ikt", first, normed).astype(BF16))
        preact = dot("cme,cmt->cet", second, spread)
        act = gelu_value(preact).astype(BF16)
        mixed = to_blocks(dot("cem,cet->cmt", third, act).astype(BF16))
        branch = dot("ikj,ikt->ijt", fourth, mixed).astype(BF16)
        return branch.reshape(width, tokens), (stream, inv, normed, spread, preact, act, mixed)

    records = [[None] * share for _ in range(sections)]
    outs = [[None] * share for _ in range(sections)]
    for layer in range(sections):
        for k in range(share):
            if layer:
                former = streams[k]
                total = waiting[k].astype(F32)
                streams[k] = (former.astype(F32) + total).astype(BF16)
                outs[layer - 1][k] = my_rows(streams[k])
            branch, records[layer][k] = forward(layer, streams[k])
            start_sum(k, branch, layer == sections - 1)

    def close_forward(k):
        outs[-1][k] = (my_rows(streams[k]).astype(F32) + waiting[k].astype(F32)).astype(BF16)

    def backward(layer, k):
        first, second, third, fourth = factors[layer]
        stream, inv, normed, spread, preact, act, mixed = records[layer][k]
        grad_blocks = grads[k].reshape(all_blocks, block_size, tokens)
        part_four = dot("ikt,ijt->ikj", mixed, grad_blocks)
        grad_mixed = to_cols(dot("ikj,ijt->ikt", fourth, grad_blocks).astype(BF16))
        part_three = dot("cet,cmt->cem", act, grad_mixed)
        grad_act = dot("cem,cmt->cet", third, grad_mixed)
        grad_pre = (grad_act * gelu_slope(preact)).astype(BF16)
        part_two = dot("cmt,cet->cme", spread, grad_pre)
        grad_spread = to_blocks(dot("cme,cet->cmt", second, grad_pre).astype(BF16))
        part_one = dot("ikt,ijt->ikj", grad_spread, normed)
        grad_norm = dot("ikj,ikt->ijt", first, grad_spread).astype(BF16)
        return grad_norm.reshape(width, tokens), (part_one, part_two, part_three, part_four)

    def norm_backward(layer, k, grad_out, grad_norm, inner_sum):
        stream, inv = records[layer][k][:2]
        gain = gains[layer]
        if inner_sum is not None:
            stream, gain = my_rows(stream), my_rows(gain)
        f = stream.astype(F32)
        grad_norm = grad_norm.astype(F32)
        scaled = grad_norm * gain[:, None]
        if inner_sum is None:
            inner_sum = jnp.sum(scaled * f, axis=0)
        result = (
            grad_out.astype(F32) + scaled * inv - f * (inv * inv * inv * inner_sum / width)
        ).astype(BF16)
        if stream.shape[0] != width_dev:
            grad_norm, f = my_rows(grad_norm), my_rows(stream).astype(F32)
        return result, jnp.sum(grad_norm * f * inv, axis=1)

    back = [[None] * share for _ in range(sections)]
    gain_parts = [0.0] * sections
    sums = [None] * sections
    inner_sums = None
    for layer in reversed(range(sections)):
        parts = []
        inner_parts = []
        for k in range(share):
            if layer == sections - 1:
                close_forward(k)
            else:
                grads[k], part_gain = norm_backward(layer + 1, k, grads[k], waiting[k], None)
                gain_parts[layer + 1] += part_gain
                back[layer + 1][k] = my_rows(grads[k])
            grad_norm, part = backward(layer, k)
            parts.append(part)
            if layer == 0:
                scaled = grad_norm.astype(F32) * gains[0][:, None]
                inner_parts.append(jnp.sum(scaled * records[0][k][0].astype(F32), axis=0))
            start_sum(k, grad_norm, layer == 0)
        if layer == 0:
            inner_sums = lax.psum(jnp.stack(inner_parts), "tensor")
        part_one, part_two, part_three, part_four = (sum(member) for member in zip(*parts))
        shape = (ranks, blocks, inner, block_size)
        ends = jnp.stack([part_one.reshape(shape), part_four.reshape(shape)], axis=1)
        sums[layer] = tuple(
            jnp.sum(quarters(member.astype(BF16)).astype(F32), axis=0).astype(BF16)
            for member in (ends, part_two, part_three)
        )
    for k in range(share):
        back[0][k], part_gain = norm_backward(0, k, my_rows(grads[k]), waiting[k], inner_sums[k])
        gain_parts[0] += part_gain

    def placed(members):
        moved = swap(jnp.stack([jnp.stack(row) for row in members]), "pipe")
        moved = moved.reshape(micro_count, width_dev, tokens)
        return moved.transpose(0, 2, 1)[None]

    def collected(which):
        moved = swap(jnp.stack([member[which] for member in sums]), "pipe")
        return moved.reshape((-1,) + moved.shape[2:])

    gain_grad = jnp.sum(swap(jnp.stack(gain_parts), "pipe"), axis=0)
    ends = swap(collected(0), "tensor")
    ends = ends.reshape(ranks, 2, blocks, expand, cols, block_size).astype(F32)
    first_grad = ends[:, 0].transpose(1, 4, 2, 0, 3)
    fourth_grad = ends[:, 1].transpose(1, 2, 0, 3, 4)
    return (
        placed(outs),
        placed(back),
        gain_grad[None],
        first_grad.reshape(1, blocks, block_size, expand * block_size),
        collected(1).astype(F32)[None],
        collected(2).astype(F32)[None],
        fourth_grad.reshape(1, blocks, expand * block_size, block_size),
    )


def solution(mesh):
    factor = P("pipe", "tensor", None, None)
    stream = P(None, None, "tensor")
    result = P("pipe", None, None, "tensor")
    return jax.shard_map(
        body,
        mesh=mesh,
        in_specs=(stream, stream, P("pipe", "tensor"), factor, factor, factor, factor),
        out_specs=(result, result, P("pipe", "tensor"), factor, factor, factor, factor),
        check_vma=False,
    )
```

time: 1840 us -> 1590 us (0.86)
  waiting for transfers between devices: 1070 us -> 660 us
  starting transfers between devices: 42.8 us -> 148 us
  local copies, waits for them, and re-layouts: 246 us -> 179 us
  blocking collectives: 111 us -> 162 us
  other arithmetic: 143 us -> 190 us
  matrix products: 192 us -> 219 us
    psum x7 -> x12, waiting for transfers between devices: 666 us -> 312 us  [start_sum(): waiting[k] = rows_first(lax.psum(partial, 'tensor'))]
    all_gather x6 -> x2, waiting for transfers between devices: 211 us -> 0.02 us  [whole_stream(): lax.all_gather(rows_first(mine), 'tensor', axis=0, tiled=True)]
    all_to_all x9 -> x33, waiting for transfers between devices: 194 us -> 334 us  [swap(): return lax.all_to_all(values, axis, split_axis=0, concat_axis=0, tiled=True)]
    reshape x27 -> x4, local copies, waits for them, and re-layouts: 133 us -> 8.56 us  [the longest x2 6.5 us: placed(): moved = moved.reshape(micro_count, width_dev, tokens)]
    all_to_all x9 -> x33, starting transfers between devices: 41 us -> 146 us  [swap(): return lax.all_to_all(values, axis, split_axis=0, concat_axis=0, tiled=True)]
    another operation x1 -> x25, local copies, waits for them, and re-layouts: 0.3 us -> 37.9 us  [the longest x12 26 us: from_quarter(): jnp.tile(values, (sections,) + (1,) * (values.ndim - 1))]
    psum x0 -> x1, blocking collectives: none -> 33.2 us  [body(): inner_sums = lax.psum(jnp.stack(inner_parts), 'tensor')]
    slice x1 -> x10, local copies, waits for them, and re-layouts: 0.01 us -> 27.5 us  [the longest x2 9.25 us: whole_stream(): return [full[:, k * tokens:(k + 1) * tokens] for k in range(share)]]
  transfers between devices with their start and end apart: 22 -> 51, of which waited for: 16 -> 37; matrix products, arithmetic and copies ran while one was open for 17% -> 34% of each run, Pallas kernels for 0% -> 0%
where the time goes in v2:
time: 1590 us; the launch traced here: 1580 us
  waiting for transfers between devices  660 us (42%)
  matrix products  219 us (14%)
  other arithmetic  190 us (12%)
  local copies, waits for them, and re-layouts  179 us (11%)
  blocking collectives  162 us (10%)
  starting transfers between devices  148 us (9%)
  between operations  17.5 us (1%)
    all_to_all x33, waiting for transfers between devices, swap(): return lax.all_to_all(values, axis, split_axis=0, concat_axis=0, tiled=True)  334 us
    psum x12, waiting for transfers between devices, start_sum(): waiting[k] = rows_first(lax.psum(partial, 'tensor'))  312 us
    dot_general x96, matrix products, dot(): return jnp.einsum(spec, left, right, preferred_element_type=F32)  219 us
    all_to_all x33, starting transfers between devices, swap(): return lax.all_to_all(values, axis, split_axis=0, concat_axis=0, tiled=True)  146 us
    all_to_all x2, blocking collectives, swap(): return lax.all_to_all(values, axis, split_axis=0, concat_axis=0, tiled=True)  102 us
    unnamed x396, local copies, waits for them, and re-layouts  56 us
    reduce_sum x12, other arithmetic, body(): jnp.sum(quarters(member.astype(BF16)).astype(F32), axis=0).astype(BF16)  34.6 us
    psum x1, blocking collectives, body(): inner_sums = lax.psum(jnp.stack(inner_parts), 'tensor')  33.2 us
  transfers between devices with their start and end apart: 51, of which 37 were waited for; matrix products, arithmetic and copies ran while one was open for 34% of the time, Pallas kernels for 0%

profile of v2, /device:TPU:0, one launch (start us, length us, event | category | flops | bytes accessed | tf_op | source)
XLA Modules:
  0.0 1576.0 jit_solution(2541744041849352167)
XLA Ops:
  7.2 31.4 %all_to_all.179 = bf16[16,256,256]{2,1,0:T(8,128)(2,1)} all-to-all(bf16[16,256,256]{2,1,0:T(8,128)(2,1)} %bitcast.723), channel_id=1, replica_groups=mesh['pipe'=4,'tensor'=8] {'pipe'}, dimensions={0} | all-to-all | bytes 4194304 | tf_op jit(solution)/shard_map/all_to_all | solution.py:33
  44.8 21.5 %all-to-all-done.2 = bf16[16,256,256]{2,1,0:T(8,128)(2,1)S(1)} async-done(((bf16[16,256,256]{2,1,0:T(8,128)(2,1)}), bf16[16,256,256]{2,1,0:T(8,128)(2,1)S(1)}, u32[]{:S(2)}, u32[]{:S(2)}) %all-to-all-start.2) | async-done | bytes 2097184 | tf_op jit(solution)/shard_map/all_to_all | solution.py:33
  80.4 16.4 %all-to-all-done.6 = bf16[16,256,256]{2,1,0:T(8,128)(2,1)} async-done(((bf16[16,256,256]{2,1,0:T(8,128)(2,1)}), bf16[16,256,256]{2,1,0:T(8,128)(2,1)}, u32[]{:S(2)}, u32[]{:S(2)}) %all-to-all-start.6) | async-done | bytes 2097184 | tf_op jit(solution)/shard_map/all_to_all | solution.py:33
  96.7 70.8 %all_to_all.180 = bf16[8,2,8,64,128]{4,3,2,1,0:T(8,128)(2,1)} all-to-all(bf16[8,2,8,64,128]{4,3,2,1,0:T(8,128)(2,1)} %copy.264), channel_id=1, replica_groups=mesh['pipe'=4,'tensor'=8] {'tensor'}, dimensions={0} | all-to-all | bytes 4194304 | tf_op jit(solution)/shard_map/all_to_all | solution.py:33
  173.1 24.1 %all-to-all-done.1 = bf16[8,2,8,64,128]{4,3,2,1,0:T(8,128)(2,1)} async-done(((bf16[8,2,8,64,128]{4,3,2,1,0:T(8,128)(2,1)}), bf16[8,2,8,64,128]{4,3,2,1,0:T(8,128)(2,1)}, u32[]{:S(2)}, u32[]{:S(2)}) %all-to-all-start.1) | async-done | bytes 2097184 | tf_op jit(solution)/shard_map/all_to_all | solution.py:33
  205.2 21.7 %all-to-all-done.5 = bf16[16,256,256]{2,1,0:T(8,128)(2,1)S(1)} async-done(((bf16[16,256,256]{2,1,0:T(8,128)(2,1)}), bf16[16,256,256]{2,1,0:T(8,128)(2,1)S(1)}, u32[]{:S(2)}, u32[]{:S(2)}) %all-to-all-start.5) | async-done | bytes 2097184 | tf_op jit(solution)/shard_map/all_to_all | solution.py:33
  234.6 14.1 all-gather
  248.7 12.7 all-gather.2
  274.9 17.8 %all-to-all-done.7 = bf16[8,2,8,64,128]{4,3,2,1,0:T(8,128)(2,1)} async-done(((bf16[8,2,8,64,128]{4,3,2,1,0:T(8,128)(2,1)}), bf16[8,2,8,64,128]{4,3,2,1,0:T(8,128)(2,1)}, u32[]{:S(2)}, u32[]{:S(2)}) %all-to-all-start.7) | async-done | bytes 2097184 | tf_op jit(solution)/shard_map/all_to_all | solution.py:33
  300.2 6.0 fusion.2
  316.9 7.2 all-to-all-done.8
  326.7 5.1 all-to-all-start.9
  347.6 8.6 all-to-all-done.9
  365.3 16.3 %all-reduce.13.cloned.1.call-done = bf16[8192,128]{1,0:T(8,128)(2,1)} async-done(((bf16[8192,128]{1,0:T(8,128)(2,1)}), bf16[8192,128]{1,0:T(8,128)(2,1)}) %all-reduce.13.cloned.1.call-update) | async-done | bytes 2097168 | tf_op jit(solution)/shard_map/psum | solution.py:86
  402.1 46.7 %all-reduce.15.cloned.1.call-done = bf16[8192,128]{1,0:T(8,128)(2,1)} async-done(((bf16[8192,128]{1,0:T(8,128)(2,1)}), bf16[8192,128]{1,0:T(8,128)(2,1)}) %all-reduce.15.cloned.1.call-update) | async-done | bytes 2097168 | tf_op jit(solution)/shard_map/psum | solution.py:86
  464.4 20.3 %all-to-all-done.11 = bf16[16,256,256]{2,1,0:T(8,128)(2,1)} async-done(((bf16[16,256,256]{2,1,0:T(8,128)(2,1)}), bf16[16,256,256]{2,1,0:T(8,128)(2,1)}, u32[]{:S(2)}, u32[]{:S(2)}) %all-to-all-start.11) | async-done | bytes 2097184 | tf_op jit(solution)/shard_map/all_to_all | solution.py:33
  507.3 9.1 all-to-all-done.12
  550.9 44.7 %all-reduce.19.cloned.1.call-done = bf16[8192,128]{1,0:T(8,128)(2,1)} async-done(((bf16[8192,128]{1,0:T(8,128)(2,1)}), bf16[8192,128]{1,0:T(8,128)(2,1)}) %all-reduce.19.cloned.1.call-update) | async-done | bytes 2097168 | tf_op jit(solution)/shard_map/psum | solution.py:86
  630.1 32.7 %all-reduce.21.cloned.1.call-done = bf16[8192,128]{1,0:T(8,128)(2,1)} async-done(((bf16[8192,128]{1,0:T(8,128)(2,1)}), bf16[8192,128]{1,0:T(8,128)(2,1)}) %all-reduce.21.cloned.1.call-update) | async-done | bytes 2097168 | tf_op jit(solution)/shard_map/psum | solution.py:86
  673.8 4.9 fusion.12
  685.2 12.2 all-to-all-done.14
  709.5 20.7 %all-reduce.23.cloned.1.call-done = bf16[8192,128]{1,0:T(8,128)(2,1)} async-done(((bf16[8192,128]{1,0:T(8,128)(2,1)}), bf16[8192,128]{1,0:T(8,128)(2,1)}) %all-reduce.23.cloned.1.call-update) | async-done | bytes 2097168 | tf_op jit(solution)/shard_map/psum | solution.py:86
  753.7 14.4 reduce-scatter.5.cloned.1.call-done
  816.2 54.5 %all-reduce.25.cloned.1.call-done = bf16[8192,128]{1,0:T(8,128)(2,1)} async-done(((bf16[8192,128]{1,0:T(8,128)(2,1)}), bf16[8192,128]{1,0:T(8,128)(2,1)}) %all-reduce.25.cloned.1.call-update) | async-done | bytes 2097168 | tf_op jit(solution)/shard_map/psum | solution.py:86
  907.5 43.0 %all-reduce.27.cloned.1.call-done = bf16[8192,128]{1,0:T(8,128)(2,1)} async-done(((bf16[8192,128]{1,0:T(8,128)(2,1)}), bf16[8192,128]{1,0:T(8,128)(2,1)}) %all-reduce.27.cloned.1.call-update) | async-done | bytes 2097168 | tf_op jit(solution)/shard_map/psum | solution.py:86
  956.2 5.4 fusion.21
  990.3 30.4 %all-reduce.29.cloned.1.call-done = bf16[8192,128]{1,0:T(8,128)(2,1)} async-done(((bf16[8192,128]{1,0:T(8,128)(2,1)}), bf16[8192,128]{1,0:T(8,128)(2,1)}) %all-reduce.29.cloned.1.call-update) | async-done | bytes 2097168 | tf_op jit(solution)/shard_map/psum | solution.py:86
  1020.8 4.7 fusion.40
  1031.4 4.8 all-to-all-start.22
  1050.2 9.8 all-to-all-done.22
  1072.2 15.5 all-reduce.31.cloned.1.call-done
  1097.1 5.0 fusion.49
  1104.9 15.7 all-to-all-done.21
  1138.7 10.8 all-to-all-done.32
  1169.8 8.7 all-to-all-done.27
  1183.2 5.1 fusion.28
  1198.0 9.5 all-to-all-done.16
  1221.2 7.3 all-reduce.35.cloned.1.call-done
  1231.4 5.0 all-to-all-done.20
  1247.3 17.9 %all-to-all-done.31 = bf16[16,256,256]{2,1,0:T(8,128)(2,1)} async-done(((bf16[16,256,256]{2,1,0:T(8,128)(2,1)}), bf16[16,256,256]{2,1,0:T(8,128)(2,1)}, u32[]{:S(2)}, u32[]{:S(2)}) %all-to-all-start.31) | async-done | bytes 2097184 | tf_op jit(solution)/shard_map/all_to_all | solution.py:33
  1265.2 4.8 all-to-all-start.26
  1283.0 11.4 all-to-all-done.26
  1304.0 19.3 %all-to-all-done.19 = bf16[8,2,8,64,128]{4,3,2,1,0:T(8,128)(2,1)} async-done(((bf16[8,2,8,64,128]{4,3,2,1,0:T(8,128)(2,1)}), bf16[8,2,8,64,128]{4,3,2,1,0:T(8,128)(2,1)}, u32[]{:S(2)}, u32[]{:S(2)}) %all-to-all-start.19) | async-done | bytes 2097184 | tf_op jit(solution)/shard_map/all_to_all | solution.py:33
  1332.2 19.9 %all-to-all-done.30 = bf16[16,256,256]{2,1,0:T(8,128)(2,1)} async-done(((bf16[16,256,256]{2,1,0:T(8,128)(2,1)}), bf16[16,256,256]{2,1,0:T(8,128)(2,1)}, u32[]{:S(2)}, u32[]{:S(2)}) %all-to-all-start.30) | async-done | bytes 2097184 | tf_op jit(solution)/shard_map/all_to_all | solution.py:33
  1400.6 9.3 all-to-all-done.23
  1428.9 9.8 all-to-all-done.34
  1449.8 17.8 %all-to-all-done.29 = bf16[4,4,256,256]{3,2,1,0:T(8,128)(2,1)} async-done(((bf16[4,4,256,256]{3,2,1,0:T(8,128)(2,1)}), bf16[4,4,256,256]{3,2,1,0:T(8,128)(2,1)}, u32[]{:S(2)}, u32[]{:S(2)}) %all-to-all-start.29) | async-done | bytes 2097184 | tf_op jit(solution)/shard_map/all_to_all | solution.py:33
  1490.9 33.2 %psum.103 = f32[2,128]{1,0:T(2,128)S(1)} all-reduce(f32[2,128]{1,0:T(2,128)S(1)} %pad_maximum_fusion.11), channel_id=1, replica_groups=mesh['pipe'=4,'tensor'=8] {'tensor'}, use_global_device_ids=true, to_apply=%region_31.0 | all-reduce | flops 256 | bytes 2048 | tf_op jit(solution)/shard_map/psum | solution.py:201
  (747 shorter events, 700.6 us)
Async XLA Ops:
  67.9 28.9 %all-to-all-start.6 = ((bf16[16,256,256]{2,1,0:T(8,128)(2,1)}), bf16[16,256,256]{2,1,0:T(8,128)(2,1)}, u32[]{:S(2)}, u32[]{:S(2)}) async-start(bf16[16,256,256]{2,1,0:T(8,128)(2,1)} %bitcast.12), calls=%async_computation.6 | async-start | bytes 4194304 | tf_op jit(solution)/shard_map/all_to_all | solution.py:33
  72.4 198.3 %all-gather.6.cloned.1.call-start = ((), (), s32[]{:S(2)}) async-start(), calls=%async_computation.39 | async-start | bytes 4718592 | tf_op jit(solution)/shard_map/all_gather | solution.py:56
  167.5 29.8 %all-to-all-start.1 = ((bf16[8,2,8,64,128]{4,3,2,1,0:T(8,128)(2,1)}), bf16[8,2,8,64,128]{4,3,2,1,0:T(8,128)(2,1)}, u32[]{:S(2)}, u32[]{:S(2)}) async-start(bf16[8,2,8,64,128]{4,3,2,1,0:T(8,128)(2,1)} %all_to_all.180), calls=%async_computation.1 | async-start | bytes 4194304 | tf_op jit(solution)/shard_map/all_to_all | solution.py:33
  228.8 32.6 %all-to-all-start.4 = ((bf16[8,2,8,64,128]{4,3,2,1,0:T(8,128)(2,1)}), bf16[8,2,8,64,128]{4,3,2,1,0:T(8,128)(2,1)}, u32[]{:S(2)}, u32[]{:S(2)}) async-start(bf16[8,2,8,64,128]{4,3,2,1,0:T(8,128)(2,1)} %bitcast.647), calls=%async_computation.4 | async-start | bytes 4194304 | tf_op jit(solution)/shard_map/all_to_all | solution.py:33
  233.4 98.4 %all-gather.8.cloned.1.call-start = ((), (), s32[]{:S(2)}) async-start(), calls=%async_computation.47 | async-start | bytes 4718592 | tf_op jit(solution)/shard_map/all_gather | solution.py:56
  263.3 29.5 %all-to-all-start.7 = ((bf16[8,2,8,64,128]{4,3,2,1,0:T(8,128)(2,1)}), bf16[8,2,8,64,128]{4,3,2,1,0:T(8,128)(2,1)}, u32[]{:S(2)}, u32[]{:S(2)}) async-start(bf16[8,2,8,64,128]{4,3,2,1,0:T(8,128)(2,1)} %bitcast.645), calls=%async_computation.7 | async-start | bytes 4194304 | tf_op jit(solution)/shard_map/all_to_all | solution.py:33
  295.3 28.9 %all-to-all-start.8 = ((bf16[16,256,256]{2,1,0:T(8,128)(2,1)}), bf16[16,256,256]{2,1,0:T(8,128)(2,1)}, u32[]{:S(2)}, u32[]{:S(2)}) async-start(bf16[16,256,256]{2,1,0:T(8,128)(2,1)} %bitcast.646), calls=%async_computation.8 | async-start | bytes 4194304 | tf_op jit(solution)/shard_map/all_to_all | solution.py:33
  299.8 81.9 %all-reduce.13.cloned.1.call-start = ((), (), s32[]{:S(2)}) async-start(), calls=%async_computation.40 | async-start | bytes 4194304 | tf_op jit(solution)/shard_map/psum | solution.py:86
  326.7 29.4 %all-to-all-start.9 = ((bf16[16,256,256]{2,1,0:T(8,128)(2,1)}), bf16[16,256,256]{2,1,0:T(8,128)(2,1)}, u32[]{:S(2)}, u32[]{:S(2)}) async-start(bf16[16,256,256]{2,1,0:T(8,128)(2,1)} %bitcast.648), calls=%async_computation.9 | async-start | bytes 4194304 | tf_op jit(solution)/shard_map/all_to_all | solution.py:33
  358.0 95.9 %all-to-all-start.10 = ((bf16[8,2,8,64,128]{4,3,2,1,0:T(8,128)(2,1)}), bf16[8,2,8,64,128]{4,3,2,1,0:T(8,128)(2,1)}, u32[]{:S(2)}, u32[]{:S(2)}) async-start(bf16[8,2,8,64,128]{4,3,2,1,0:T(8,128)(2,1)} %bitcast.59), calls=%async_computation.10 | async-start | bytes 4194304 | tf_op jit(solution)/shard_map/all_to_all | solution.py:33
  362.5 86.3 %all-reduce.15.cloned.1.call-start = ((), (), s32[]{:S(2)}) async-start(), calls=%async_computation.41 | async-start | bytes 4194304 | tf_op jit(solution)/shard_map/psum | solution.py:86
  381.7 149.4 %all-reduce.17.cloned.1.call-start = ((), (), s32[]{:S(2)}) async-start(), calls=%async_computation.42 | async-start | bytes 4194304 | tf_op jit(solution)/shard_map/psum | solution.py:86
  456.5 28.2 %all-to-all-start.11 = ((bf16[16,256,256]{2,1,0:T(8,128)(2,1)}), bf16[16,256,256]{2,1,0:T(8,128)(2,1)}, u32[]{:S(2)}, u32[]{:S(2)}) async-start(bf16[16,256,256]{2,1,0:T(8,128)(2,1)} %bitcast.652), calls=%async_computation.11 | async-start | bytes 4194304 | tf_op jit(solution)/shard_map/all_to_all | solution.py:33
  487.3 29.1 %all-to-all-start.12 = ((bf16[16,256,256]{2,1,0:T(8,128)(2,1)}), bf16[16,256,256]{2,1,0:T(8,128)(2,1)}, u32[]{:S(2)}, u32[]{:S(2)}) async-start(bf16[16,256,256]{2,1,0:T(8,128)(2,1)} %bitcast.649), calls=%async_computation.12 | async-start | bytes 4194304 | tf_op jit(solution)/shard_map/all_to_all | solution.py:33
  523.4 92.2 %all-to-all-start.13 = ((bf16[8,2,8,64,128]{4,3,2,1,0:T(8,128)(2,1)}), bf16[8,2,8,64,128]{4,3,2,1,0:T(8,128)(2,1)}, u32[]{:S(2)}, u32[]{:S(2)}) async-start(bf16[8,2,8,64,128]{4,3,2,1,0:T(8,128)(2,1)} %bitcast.644), calls=%async_computation.13 | async-start | bytes 4194304 | tf_op jit(solution)/shard_map/all_to_all | solution.py:33
  527.8 67.8 %all-reduce.19.cloned.1.call-start = ((), (), s32[]{:S(2)}) async-start(), calls=%async_computation.43 | async-start | bytes 4194304 | tf_op jit(solution)/shard_map/psum | solution.py:86
  531.1 131.7 %all-reduce.21.cloned.1.call-start = ((), (), s32[]{:S(2)}) async-start(), calls=%async_computation.44 | async-start | bytes 4194304 | tf_op jit(solution)/shard_map/psum | solution.py:86
  617.1 49.6 %all-to-all-start.15 = ((bf16[16,256,256]{1,2,0:T(8,128)(2,1)}), bf16[16,256,256]{1,2,0:T(8,128)(2,1)}, u32[]{:S(2)}, u32[]{:S(2)}) async-start(bf16[16,256,256]{1,2,0:T(8,128)(2,1)} %bitcast.87), calls=%async_computation.15 | async-start | bytes 4194304 | tf_op jit(solution)/shard_map/all_to_all | solution.py:33
  621.6 108.6 %all-reduce.23.cloned.1.call-start = ((), (), s32[]{:S(2)}) async-start(), calls=%async_computation.45 | async-start | bytes 4194304 | tf_op jit(solution)/shard_map/psum | solution.py:86
  669.3 28.1 %all-to-all-start.14 = ((bf16[16,256,256]{1,2,0:T(8,128)(2,1)}), bf16[16,256,256]{1,2,0:T(8,128)(2,1)}, u32[]{:S(2)}, u32[]{:S(2)}) async-start(bf16[16,256,256]{1,2,0:T(8,128)(2,1)} %bitcast.650), calls=%async_computation.14 | async-start | bytes 4194304 | tf_op jit(solution)/shard_map/all_to_all | solution.py:33
  673.8 94.2 %reduce-scatter.5.cloned.1.call-start = ((), (), s32[]{:S(2)}) async-start(), calls=%async_computation.46 | async-start | bytes 2359296 | tf_op jit(solution)/shard_map/reduce_scatter | solution.py:84
  730.2 75.8 %reduce-scatter.7.cloned.1.call-start = ((), (), s32[]{:S(2)}) async-start(), calls=%async_computation.48 | async-start | bytes 2359296 | tf_op jit(solution)/shard_map/reduce_scatter | solution.py:84
  785.6 245.8 %all-to-all-start.33 = ((bf16[16,256,256]{2,1,0:T(8,128)(2,1)}), bf16[16,256,256]{2,1,0:T(8,128)(2,1)}, u32[]{:S(2)}, u32[]{:S(2)}) async-start(bf16[16,256,256]{2,1,0:T(8,128)(2,1)} %add_convert_fusion), calls=%async_computation.37 | async-start | bytes 4194304 | tf_op jit(solution)/shard_map/all_to_all | solution.py:33
  790.1 80.6 %all-reduce.25.cloned.1.call-start = ((), (), s32[]{:S(2)}) async-start(), calls=%async_computation.49 | async-start | bytes 4194304 | tf_op jit(solution)/shard_map/psum | solution.py:86
  806.0 144.5 %all-reduce.27.cloned.1.call-start = ((), (), s32[]{:S(2)}) async-start(), calls=%async_computation.50 | async-start | bytes 4194304 | tf_op jit(solution)/shard_map/psum | solution.py:86
  885.8 135.0 %all-reduce.29.cloned.1.call-start = ((), (), s32[]{:S(2)}) async-start(), calls=%async_computation.51 | async-start | bytes 4194304 | tf_op jit(solution)/shard_map/psum | solution.py:86
  955.9 131.8 %all-reduce.31.cloned.1.call-start = ((), (), s32[]{:S(2)}) async-start(), calls=%async_computation.52 | async-start | bytes 4194304 | tf_op jit(solution)/shard_map/psum | solution.py:86
  1031.4 28.5 %all-to-all-start.22 = ((bf16[8,2,8,64,128]{4,3,2,1,0:T(8,128)(2,1)}), bf16[8,2,8,64,128]{4,3,2,1,0:T(8,128)(2,1)}, u32[]{:S(2)}, u32[]{:S(2)}) async-start(bf16[8,2,8,64,128]{4,3,2,1,0:T(8,128)(2,1)} %pad_maximum_fusion.6), calls=%async_computation.26 | async-start | bytes 4194304 | tf_op jit(solution)/shard_map/all_to_all | solution.py:33
  1060.0 32.4 %all-to-all-start.28 = ((bf16[16,256,256]{2,1,0:T(8,128)(2,1)}), bf16[16,256,256]{2,1,0:T(8,128)(2,1)}, u32[]{:S(2)}, u32[]{:S(2)}) async-start(bf16[16,256,256]{2,1,0:T(8,128)(2,1)} %add_convert_fusion.4), calls=%async_computation.32 | async-start | bytes 4194304 | tf_op jit(solution)/shard_map/all_to_all | solution.py:33
  1064.4 99.1 %all-reduce.33.cloned.1.call-start = ((), (), s32[]{:S(2)}) async-start(), calls=%async_computation.53 | async-start | bytes 4194304 | tf_op jit(solution)/shard_map/psum | solution.py:86
  1092.4 28.2 %all-to-all-start.21 = ((bf16[8,2,8,64,128]{4,3,2,1,0:T(8,128)(2,1)}), bf16[8,2,8,64,128]{4,3,2,1,0:T(8,128)(2,1)}, u32[]{:S(2)}, u32[]{:S(2)}) async-start(bf16[8,2,8,64,128]{4,3,2,1,0:T(8,128)(2,1)} %pad_maximum_fusion.5), calls=%async_computation.25 | async-start | bytes 4194304 | tf_op jit(solution)/shard_map/all_to_all | solution.py:33
  1120.6 28.9 %all-to-all-start.32 = ((bf16[16,256,256]{2,1,0:T(8,128)(2,1)}), bf16[16,256,256]{2,1,0:T(8,128)(2,1)}, u32[]{:S(2)}, u32[]{:S(2)}) async-start(bf16[16,256,256]{2,1,0:T(8,128)(2,1)} %add_convert_fusion.1), calls=%async_computation.36 | async-start | bytes 4194304 | tf_op jit(solution)/shard_map/all_to_all | solution.py:33
  1149.5 29.0 %all-to-all-start.27 = ((bf16[16,256,256]{2,1,0:T(8,128)(2,1)}), bf16[16,256,256]{2,1,0:T(8,128)(2,1)}, u32[]{:S(2)}, u32[]{:S(2)}) async-start(bf16[16,256,256]{2,1,0:T(8,128)(2,1)} %add_convert_fusion.5), calls=%async_computation.31 | async-start | bytes 4194304 | tf_op jit(solution)/shard_map/all_to_all | solution.py:33
  1154.1 74.4 %all-reduce.35.cloned.1.call-start = ((), (), s32[]{:S(2)}) async-start(), calls=%async_computation.54 | async-start | bytes 4194304 | tf_op jit(solution)/shard_map/psum | solution.py:86
  1178.5 29.0 %all-to-all-start.16 = ((bf16[4,2,1024,128]{3,2,1,0:T(8,128)(2,1)}), bf16[4,2,1024,128]{3,2,1,0:T(8,128)(2,1)}, u32[]{:S(2)}, u32[]{:S(2)}) async-start(bf16[4,2,1024,128]{3,2,1,0:T(8,128)(2,1)} %pad_maximum_fusion.1), calls=%async_computation.18 | async-start | bytes 4194304 | tf_op jit(solution)/shard_map/all_to_all | solution.py:33
  1207.5 28.9 %all-to-all-start.20 = ((bf16[8,2,8,64,128]{4,3,2,1,0:T(8,128)(2,1)}), bf16[8,2,8,64,128]{4,3,2,1,0:T(8,128)(2,1)}, u32[]{:S(2)}, u32[]{:S(2)}) async-start(bf16[8,2,8,64,128]{4,3,2,1,0:T(8,128)(2,1)} %pad_maximum_fusion.4), calls=%async_computation.24 | async-start | bytes 4194304 | tf_op jit(solution)/shard_map/all_to_all | solution.py:33
  1236.4 28.8 %all-to-all-start.31 = ((bf16[16,256,256]{2,1,0:T(8,128)(2,1)}), bf16[16,256,256]{2,1,0:T(8,128)(2,1)}, u32[]{:S(2)}, u32[]{:S(2)}) async-start(bf16[16,256,256]{2,1,0:T(8,128)(2,1)} %add_convert_fusion.2), calls=%async_computation.35 | async-start | bytes 4194304 | tf_op jit(solution)/shard_map/all_to_all | solution.py:33
  1265.2 29.2 %all-to-all-start.26 = ((bf16[16,256,256]{2,1,0:T(8,128)(2,1)}), bf16[16,256,256]{2,1,0:T(8,128)(2,1)}, u32[]{:S(2)}, u32[]{:S(2)}) async-start(bf16[16,256,256]{2,1,0:T(8,128)(2,1)} %add_convert_fusion.6), calls=%async_computation.30 | async-start | bytes 4194304 | tf_op jit(solution)/shard_map/all_to_all | solution.py:33
  1294.4 28.9 %all-to-all-start.19 = ((bf16[8,2,8,64,128]{4,3,2,1,0:T(8,128)(2,1)}), bf16[8,2,8,64,128]{4,3,2,1,0:T(8,128)(2,1)}, u32[]{:S(2)}, u32[]{:S(2)}) async-start(bf16[8,2,8,64,128]{4,3,2,1,0:T(8,128)(2,1)} %pad_maximum_fusion.3), calls=%async_computation.23 | async-start | bytes 4194304 | tf_op jit(solution)/shard_map/all_to_all | solution.py:33
  1323.3 28.8 %all-to-all-start.30 = ((bf16[16,256,256]{2,1,0:T(8,128)(2,1)}), bf16[16,256,256]{2,1,0:T(8,128)(2,1)}, u32[]{:S(2)}, u32[]{:S(2)}) async-start(bf16[16,256,256]{2,1,0:T(8,128)(2,1)} %add_convert_fusion.3), calls=%async_computation.34 | async-start | bytes 4194304 | tf_op jit(solution)/shard_map/all_to_all | solution.py:33
  1352.1 28.9 %all-to-all-start.25 = ((bf16[16,256,256]{2,1,0:T(8,128)(2,1)}), bf16[16,256,256]{2,1,0:T(8,128)(2,1)}, u32[]{:S(2)}, u32[]{:S(2)}) async-start(bf16[16,256,256]{2,1,0:T(8,128)(2,1)} %add_convert_fusion.7), calls=%async_computation.29 | async-start | bytes 4194304 | tf_op jit(solution)/shard_map/all_to_all | solution.py:33
  1381.0 28.9 %all-to-all-start.23 = ((bf16[4,2,2,8,64,128]{5,4,3,1,2,0:T(8,128)(2,1)}), bf16[4,2,2,8,64,128]{5,4,3,1,2,0:T(8,128)(2,1)}, u32[]{:S(2)}, u32[]{:S(2)}) async-start(bf16[4,2,2,8,64,128]{5,4,3,1,2,0:T(8,128)(2,1)} %pad_maximum_fusion.7), calls=%async_computation.27 | async-start | bytes 4194304 | tf_op jit(solution)/shard_map/all_to_all | solution.py:33
  1385.5 64.3 %reduce-scatter.9.cloned.1.call-start = ((), (), s32[]{:S(2)}) async-start(), calls=%async_computation.55 | async-start | bytes 2359296 | tf_op jit(solution)/shard_map/reduce_scatter | solution.py:84
  1409.8 28.8 %all-to-all-start.34 = ((bf16[4,4,256,256]{3,2,1,0:T(8,128)(2,1)}), bf16[4,4,256,256]{3,2,1,0:T(8,128)(2,1)}, u32[]{:S(2)}, u32[]{:S(2)}) async-start(bf16[4,4,256,256]{3,2,1,0:T(8,128)(2,1)} %pad_maximum_fusion.9), calls=%async_computation.38 | async-start | bytes 4194304 | tf_op jit(solution)/shard_map/all_to_all | solution.py:33
  1438.7 28.9 %all-to-all-start.29 = ((bf16[4,4,256,256]{3,2,1,0:T(8,128)(2,1)}), bf16[4,4,256,256]{3,2,1,0:T(8,128)(2,1)}, u32[]{:S(2)}, u32[]{:S(2)}) async-start(bf16[4,4,256,256]{3,2,1,0:T(8,128)(2,1)} %pad_maximum_fusion.8), calls=%async_computation.33 | async-start | bytes 4194304 | tf_op jit(solution)/shard_map/all_to_all | solution.py:33
  1443.2 83.6 %reduce-scatter.11.cloned.1.call-start = ((), (), s32[]{:S(2)}) async-start(), calls=%async_computation.56 | async-start | bytes 2359296 | tf_op jit(solution)/shard_map/reduce_scatter | solution.py:84
  1467.6 61.5 %all-to-all-start.24 = ((bf16[8,2,8,64,128]{4,3,2,1,0:T(8,128)(2,1)}), bf16[8,2,8,64,128]{4,3,2,1,0:T(8,128)(2,1)}, u32[]{:S(2)}, u32[]{:S(2)}) async-start(bf16[8,2,8,64,128]{4,3,2,1,0:T(8,128)(2,1)} %bitcast.653), calls=%async_computation.28 | async-start | bytes 4194304 | tf_op jit(solution)/shard_map/all_to_all | solution.py:33
  1537.4 29.0 %all-to-all-start.17 = ((bf16[4,2,1024,128]{3,2,1,0:T(8,128)(2,1)}), bf16[4,2,1024,128]{3,2,1,0:T(8,128)(2,1)S(1)}, u32[]{:S(2)}, u32[]{:S(2)}) async-start(bf16[4,2,1024,128]{3,2,1,0:T(8,128)(2,1)} %pad_maximum_fusion.2), calls=%async_computation.21 | async-start | bytes 4194304 | tf_op jit(solution)/shard_map/all_to_all | solution.py:33
  (198 other events, 1654.7 us)
Sparse Core Ops, SparseCore 0:
  75.7 72.0 all-gather.5
  235.9 46.7 all-gather.7
  317.1 64.5 all-reduce.12
  384.4 64.3 all-reduce.14
  451.0 64.8 all-reduce.16
  531.3 64.3 all-reduce.18
  598.0 64.7 all-reduce.20
  665.7 64.3 all-reduce.22
  732.5 35.4 reduce-scatter.4
  770.1 34.4 reduce-scatter.6
  807.0 63.6 all-reduce.24
  885.9 64.5 all-reduce.26
  956.0 64.6 all-reduce.28
  1022.9 64.7 all-reduce.30
  1089.9 64.4 all-reduce.32
  1163.7 64.7 all-reduce.34
  1388.3 35.3 reduce-scatter.8
  1449.9 38.9 reduce-scatter.10

commit v3 on v2

--- a/solution.py
+++ b/solution.py
@@ -4,6 +4,7 @@
 import jax.numpy as jnp
 from jax import lax
 from jax.experimental.layout import Layout, with_layout_constraint
+from jax.sharding import Mesh
 from jax.sharding import PartitionSpec as P
 
 EPS = 1e-05
@@ -13,6 +14,9 @@
 BF16 = jnp.bfloat16
 
 
+TENSOR = ("chip", "core")
+
+
 def gelu_value(preact):
     tanh_val = jnp.tanh(TANH_SCALE * (preact + CUBIC_COEF * preact * preact * preact))
     return 0.5 * preact * (1.0 + tanh_val)
@@ -36,8 +40,8 @@
 def body(inputs, cotangent, norm_gain, first_factor, second_factor, third_factor, fourth_factor):
     sections = lax.axis_size("pipe")
     group = lax.axis_index("pipe")
-    ranks = lax.axis_size("tensor")
-    rank = lax.axis_index("tensor")
+    ranks = lax.axis_size(TENSOR)
+    rank = lax.axis_index(TENSOR)
     micro_count, tokens, width_dev = inputs.shape
     width = width_dev * ranks
     share = micro_count // sections
@@ -53,7 +57,7 @@
     def whole_stream(values):
         mine = lax.dynamic_slice_in_dim(values, group * share, share, 0)
         mine = mine.reshape(share * tokens, width_dev).T
-        full = rows_first(lax.all_gather(rows_first(mine), "tensor", axis=0, tiled=True))
+        full = rows_first(lax.all_gather(rows_first(mine), TENSOR, axis=0, tiled=True))
         return [full[:, k * tokens : (k + 1) * tokens] for k in range(share)]
 
     def to_cols(values):
@@ -76,15 +80,34 @@
     waiting = [None] * share
     newest = [None]
 
-    def start_sum(k, partial, scatter):
+    core = lax.axis_index("core")
+    chips = lax.axis_size("chip")
+
+    def from_other_core(values):
+        return lax.ppermute(values, "core", [(0, 1), (1, 0)])
+
+    def start_sum(k, partial, scatter, riders=()):
+        halves = partial.reshape(chips, 2, width_dev, tokens)
+        kept = lax.dynamic_index_in_dim(halves, core, 1, keepdims=False)
+        sent = lax.dynamic_index_in_dim(halves, 1 - core, 1, keepdims=False)
+        kept = (kept.astype(F32) + from_other_core(sent).astype(F32)).astype(BF16)
+        kept = kept.reshape(chips * width_dev, tokens)
         if newest[0] is not None:
             last = newest[0]
-            partial, waiting[last] = lax.optimization_barrier((partial, waiting[last]))
+            kept, waiting[last], riders = lax.optimization_barrier((kept, waiting[last], riders))
         if scatter:
-            waiting[k] = lax.psum_scatter(partial, "tensor", scatter_dimension=0, tiled=True)
+            waiting[k] = lax.psum_scatter(kept, "chip", scatter_dimension=0, tiled=True)
         else:
-            waiting[k] = rows_first(lax.psum(partial, "tensor"))
+            waiting[k] = rows_first(lax.psum(kept, "chip"))
         newest[0] = k
+        return riders
+
+    def finished(k):
+        mine = waiting[k].reshape(chips, width_dev, tokens)
+        other = from_other_core(mine)
+        is_even = core == 0
+        both = (jnp.where(is_even, mine, other), jnp.where(is_even, other, mine))
+        return jnp.stack(both, axis=1).reshape(width, tokens)
 
     def quarters(values):
         moved = swap(values, "pipe")
@@ -97,7 +120,7 @@
     first = first.transpose(3, 0, 2, 4, 1).reshape(ranks, blocks, inner, block_size)
     fourth = fourth_factor[0].reshape(blocks, expand, ranks, cols, block_size)
     fourth = fourth.transpose(2, 0, 1, 3, 4).reshape(ranks, blocks, inner, block_size)
-    outer = quarters(swap(jnp.stack([first, fourth], axis=1), "tensor"))
+    outer = quarters(swap(jnp.stack([first, fourth], axis=1), TENSOR))
     second = quarters(second_factor[0])
     third = quarters(third_factor[0])
     weights = []
@@ -114,8 +137,8 @@
 
     streams = whole_stream(inputs)
     grads = whole_stream(cotangent)
-    gains = lax.all_gather(norm_gain[0], "tensor", axis=0, tiled=True)
-    gains = lax.all_gather(gains, "pipe", axis=0, tiled=False)
+    gains = lax.all_gather(norm_gain[0], ("pipe",) + TENSOR, axis=0, tiled=True)
+    gains = gains.reshape(sections, width)
 
     def forward(layer, stream):
         first, second, third, fourth = factors[layer]
@@ -136,7 +159,7 @@
         for k in range(share):
             if layer:
                 former = streams[k]
-                total = waiting[k].astype(F32)
+                total = finished(k).astype(F32)
                 streams[k] = (former.astype(F32) + total).astype(BF16)
                 outs[layer - 1][k] = my_rows(streams[k])
             branch, records[layer][k] = forward(layer, streams[k])
@@ -160,45 +183,34 @@
         grad_norm = dot("ikj,ikt->ijt", first, grad_spread).astype(BF16)
         return grad_norm.reshape(width, tokens), (part_one, part_two, part_three, part_four)
 
-    def norm_backward(layer, k, grad_out, grad_norm, inner_sum):
+    def norm_backward(layer, k):
         stream, inv = records[layer][k][:2]
-        gain = gains[layer]
-        if inner_sum is not None:
-            stream, gain = my_rows(stream), my_rows(gain)
         f = stream.astype(F32)
-        grad_norm = grad_norm.astype(F32)
-        scaled = grad_norm * gain[:, None]
-        if inner_sum is None:
-            inner_sum = jnp.sum(scaled * f, axis=0)
-        result = (
-            grad_out.astype(F32) + scaled * inv - f * (inv * inv * inv * inner_sum / width)
+        grad_norm = finished(k).astype(F32)
+        scaled = grad_norm * gains[layer][:, None]
+        inner_sum = jnp.sum(scaled * f, axis=0)
+        grads[k] = (
+            grads[k].astype(F32) + scaled * inv - f * (inv * inv * inv * inner_sum / width)
         ).astype(BF16)
-        if stream.shape[0] != width_dev:
-            grad_norm, f = my_rows(grad_norm), my_rows(stream).astype(F32)
-        return result, jnp.sum(grad_norm * f * inv, axis=1)
+        back[layer][k] = my_rows(grads[k])
+        gain_parts[layer] += jnp.sum(my_rows(grad_norm) * my_rows(stream).astype(F32) * inv, axis=1)
 
     back = [[None] * share for _ in range(sections)]
     gain_parts = [0.0] * sections
-    sums = [None] * sections
-    inner_sums = None
+    sums = [()] * (sections + 1)
     for layer in reversed(range(sections)):
         parts = []
-        inner_parts = []
         for k in range(share):
             if layer == sections - 1:
                 close_forward(k)
             else:
-                grads[k], part_gain = norm_backward(layer + 1, k, grads[k], waiting[k], None)
-                gain_parts[layer + 1] += part_gain
-                back[layer + 1][k] = my_rows(grads[k])
+                norm_backward(layer + 1, k)
             grad_norm, part = backward(layer, k)
             parts.append(part)
-            if layer == 0:
-                scaled = grad_norm.astype(F32) * gains[0][:, None]
-                inner_parts.append(jnp.sum(scaled * records[0][k][0].astype(F32), axis=0))
-            start_sum(k, grad_norm, layer == 0)
-        if layer == 0:
-            inner_sums = lax.psum(jnp.stack(inner_parts), "tensor")
+            if k == share - 1:
+                sums[layer + 1] = start_sum(k, grad_norm, False, sums[layer + 1])
+            else:
+                start_sum(k, grad_norm, False)
         part_one, part_two, part_three, part_four = (sum(member) for member in zip(*parts))
         shape = (ranks, blocks, inner, block_size)
         ends = jnp.stack([part_one.reshape(shape), part_four.reshape(shape)], axis=1)
@@ -206,9 +218,9 @@
             jnp.sum(quarters(member.astype(BF16)).astype(F32), axis=0).astype(BF16)
             for member in (ends, part_two, part_three)
         )
+    sums = sums[:sections]
     for k in range(share):
-        back[0][k], part_gain = norm_backward(0, k, my_rows(grads[k]), waiting[k], inner_sums[k])
-        gain_parts[0] += part_gain
+        norm_backward(0, k)
 
     def placed(members):
         moved = swap(jnp.stack([jnp.stack(row) for row in members]), "pipe")
@@ -220,7 +232,7 @@
         return moved.reshape((-1,) + moved.shape[2:])
 
     gain_grad = jnp.sum(swap(jnp.stack(gain_parts), "pipe"), axis=0)
-    ends = swap(collected(0), "tensor")
+    ends = swap(collected(0), TENSOR)
     ends = ends.reshape(ranks, 2, blocks, expand, cols, block_size).astype(F32)
     first_grad = ends[:, 0].transpose(1, 4, 2, 0, 3)
     fourth_grad = ends[:, 1].transpose(1, 2, 0, 3, 4)
@@ -236,13 +248,15 @@
 
 
 def solution(mesh):
-    factor = P("pipe", "tensor", None, None)
-    stream = P(None, None, "tensor")
-    result = P("pipe", None, None, "tensor")
+    pipes, ranks = mesh.shape["pipe"], mesh.shape["tensor"]
+    split = Mesh(mesh.devices.reshape(pipes, ranks // 2, 2), ("pipe",) + TENSOR)
+    factor = P("pipe", TENSOR, None, None)
+    stream = P(None, None, TENSOR)
+    result = P("pipe", None, None, TENSOR)
     return jax.shard_map(
         body,
-        mesh=mesh,
-        in_specs=(stream, stream, P("pipe", "tensor"), factor, factor, factor, factor),
-        out_specs=(result, result, P("pipe", "tensor"), factor, factor, factor, factor),
+        mesh=split,
+        in_specs=(stream, stream, P("pipe", TENSOR), factor, factor, factor, factor),
+        out_specs=(result, result, P("pipe", TENSOR), factor, factor, factor, factor),
         check_vma=False,
     )

time: 1590 us -> 1900 us (1.19)
  waiting for transfers between devices: 660 us -> 984 us
  blocking collectives: 162 us -> 73.9 us
  other arithmetic: 190 us -> 230 us
  local copies, waits for them, and re-layouts: 179 us -> 203 us
    psum x12 -> x14, waiting for transfers between devices: 312 us -> 482 us  [start_sum(): waiting[k] = rows_first(lax.psum(kept, 'chip'))]
    all_to_all x33 -> x34, waiting for transfers between devices: 334 us -> 475 us  [swap(): return lax.all_to_all(values, axis, split_axis=0, concat_axis=0, tiled=True)]
    all_to_all x2 -> x1, blocking collectives: 102 us -> 31.4 us  [swap(): return lax.all_to_all(values, axis, split_axis=0, concat_axis=0, tiled=True)]
    psum x1 -> x0, blocking collectives: 33.2 us -> none  [body(): inner_sums = lax.psum(jnp.stack(inner_parts), 'tensor')]
    convert_element_type x12 -> x36, other arithmetic: 33.5 us -> 65.4 us  [the longest x16 37.1 us: start_sum(): kept = (kept.astype(F32) + from_other_core(sent).astype(F32)).astype(BF16)]
    all_gather x2 -> x1, blocking collectives: 26.9 us -> 42.6 us  [body(): gains = lax.all_gather(norm_gain[0], ('pipe',) + TENSOR, axis=0, tiled=True)]
    unnamed x396 -> x463, local copies, waits for them, and re-layouts: 56 us -> 64.7 us
    all_to_all x33 -> x34, starting transfers between devices: 146 us -> 150 us  [swap(): return lax.all_to_all(values, axis, split_axis=0, concat_axis=0, tiled=True)]
  transfers between devices with their start and end apart: 51 -> 82, of which waited for: 37 -> 49; matrix products, arithmetic and copies ran while one was open for 34% -> 27% of each run, Pallas kernels for 0% -> 0%
where the time goes in v3:
time: 1900 us; the launch traced here: 1890 us
  waiting for transfers between devices  984 us (52%)
  other arithmetic  230 us (12%)
  matrix products  220 us (12%)
  local copies, waits for them, and re-layouts  203 us (11%)
  starting transfers between devices  156 us (8%)
  blocking collectives  73.9 us (4%)
    psum x14, waiting for transfers between devices, start_sum(): waiting[k] = rows_first(lax.psum(kept, 'chip'))  482 us
    all_to_all x34, waiting for transfers between devices, swap(): return lax.all_to_all(values, axis, split_axis=0, concat_axis=0, tiled=True)  475 us
    dot_general x96, matrix products, dot(): return jnp.einsum(spec, left, right, preferred_element_type=F32)  220 us
    all_to_all x34, starting transfers between devices, swap(): return lax.all_to_all(values, axis, split_axis=0, concat_axis=0, tiled=True)  150 us
    unnamed x463, local copies, waits for them, and re-layouts  64.7 us
    all_gather x1, blocking collectives, body(): gains = lax.all_gather(norm_gain[0], ('pipe',) + TENSOR, axis=0, tiled=True)  42.6 us
  transfers between devices with their start and end apart: 82, of which 49 were waited for; matrix products, arithmetic and copies ran while one was open for 27% of the time, Pallas kernels for 0%

profile of v3, /device:TPU:0, one launch (start us, length us, event | category | flops | bytes accessed | tf_op | source)
XLA Modules:
  0.0 1885.0 jit_solution(7013793534431665549)
XLA Ops:
  7.2 31.4 %all_to_all.179 = bf16[16,256,256]{2,1,0:T(8,128)(2,1)} all-to-all(bf16[16,256,256]{2,1,0:T(8,128)(2,1)} %bitcast.984), channel_id=1, replica_groups=mesh['pipe'=4,'chip'=4,'core'=2] {'pipe'}, dimensions={0} | all-to-all | bytes 4194304 | tf_op jit(solution)/shard_map/all_to_all | solution.py:37
  44.8 21.5 %all-to-all-done.2 = bf16[16,256,256]{2,1,0:T(8,128)(2,1)S(1)} async-done(((bf16[16,256,256]{2,1,0:T(8,128)(2,1)}), bf16[16,256,256]{2,1,0:T(8,128)(2,1)S(1)}, u32[]{:S(2)}, u32[]{:S(2)}) %all-to-all-start.2) | async-done | bytes 2097184 | tf_op jit(solution)/shard_map/all_to_all | solution.py:37
  77.2 19.5 %all-to-all-done.6 = bf16[16,256,256]{2,1,0:T(8,128)(2,1)} async-done(((bf16[16,256,256]{2,1,0:T(8,128)(2,1)}), bf16[16,256,256]{2,1,0:T(8,128)(2,1)}, u32[]{:S(2)}, u32[]{:S(2)}) %all-to-all-start.6) | async-done | bytes 2097184 | tf_op jit(solution)/shard_map/all_to_all | solution.py:37
  104.5 79.3 %all-to-all-done = bf16[8,2,8,64,128]{4,3,2,1,0:T(8,128)(2,1)} async-done(((bf16[8,2,8,64,128]{4,3,2,1,0:T(8,128)(2,1)}), bf16[8,2,8,64,128]{4,3,2,1,0:T(8,128)(2,1)}, u32[]{:S(2)}, u32[]{:S(2)}) %all-to-all-start) | async-done | bytes 2097184 | tf_op jit(solution)/shard_map/all_to_all | solution.py:37
  189.5 22.9 %all-to-all-done.1 = bf16[8,2,8,64,128]{4,3,2,1,0:T(8,128)(2,1)} async-done(((bf16[8,2,8,64,128]{4,3,2,1,0:T(8,128)(2,1)}), bf16[8,2,8,64,128]{4,3,2,1,0:T(8,128)(2,1)}, u32[]{:S(2)}, u32[]{:S(2)}) %all-to-all-start.1) | async-done | bytes 2097184 | tf_op jit(solution)/shard_map/all_to_all | solution.py:37
  217.7 42.6 %all-gather = f32[1,32768]{1,0:T(1,128)S(1)} all-gather(f32[1,1024]{1,0:T(1,128)S(1)} %copy-done.213), channel_id=2, replica_groups=mesh['pipe'=4,'chip'=4,'core'=2] {'pipe','chip','core'}, dimensions={1}, use_global_device_ids=true | all-gather | bytes 135168 | tf_op jit(solution)/shard_map/all_gather | solution.py:140
  269.5 25.7 %all-to-all-done.4 = bf16[8,2,8,64,128]{4,3,2,1,0:T(8,128)(2,1)} async-done(((bf16[8,2,8,64,128]{4,3,2,1,0:T(8,128)(2,1)}), bf16[8,2,8,64,128]{4,3,2,1,0:T(8,128)(2,1)}, u32[]{:S(2)}, u32[]{:S(2)}) %all-to-all-start.4) | async-done | bytes 2097184 | tf_op jit(solution)/shard_map/all_to_all | solution.py:37
  346.3 11.8 all-to-all-done.8
  366.6 30.2 %all-reduce.15.cloned.1.call-done = bf16[4096,128]{1,0:T(8,128)(2,1)} async-done(((bf16[4096,128]{1,0:T(8,128)(2,1)}), bf16[4096,128]{1,0:T(8,128)(2,1)}) %all-reduce.15.cloned.1.call-update) | async-done | bytes 1048592 | tf_op jit(solution)/shard_map/psum | solution.py:101
  426.2 45.8 %all-reduce.17.cloned.1.call-done = bf16[4096,128]{1,0:T(8,128)(2,1)} async-done(((bf16[4096,128]{1,0:T(8,128)(2,1)}), bf16[4096,128]{1,0:T(8,128)(2,1)}) %all-reduce.17.cloned.1.call-update) | async-done | bytes 1048592 | tf_op jit(solution)/shard_map/psum | solution.py:101
  474.9 4.9 all-to-all-start.10
  490.5 15.1 all-to-all-done.10
  523.4 14.3 all-to-all-done.11
  546.7 28.6 %all-reduce.19.cloned.1.call-done = bf16[4096,128]{1,0:T(8,128)(2,1)} async-done(((bf16[4096,128]{1,0:T(8,128)(2,1)}), bf16[4096,128]{1,0:T(8,128)(2,1)}) %all-reduce.19.cloned.1.call-update) | async-done | bytes 1048592 | tf_op jit(solution)/shard_map/psum | solution.py:101
  602.6 46.1 %all-reduce.21.cloned.1.call-done = bf16[4096,128]{1,0:T(8,128)(2,1)} async-done(((bf16[4096,128]{1,0:T(8,128)(2,1)}), bf16[4096,128]{1,0:T(8,128)(2,1)}) %all-reduce.21.cloned.1.call-update) | async-done | bytes 1048592 | tf_op jit(solution)/shard_map/psum | solution.py:101
  678.7 45.8 %all-reduce.23.cloned.1.call-done = bf16[4096,128]{1,0:T(8,128)(2,1)} async-done(((bf16[4096,128]{1,0:T(8,128)(2,1)}), bf16[4096,128]{1,0:T(8,128)(2,1)}) %all-reduce.23.cloned.1.call-update) | async-done | bytes 1048592 | tf_op jit(solution)/shard_map/psum | solution.py:101
  736.3 21.1 %all-to-all-done.13 = bf16[8,2,8,64,128]{4,3,2,1,0:T(8,128)(2,1)} async-done(((bf16[8,2,8,64,128]{4,3,2,1,0:T(8,128)(2,1)}), bf16[8,2,8,64,128]{4,3,2,1,0:T(8,128)(2,1)}, u32[]{:S(2)}, u32[]{:S(2)}) %all-to-all-start.13) | async-done | bytes 2097184 | tf_op jit(solution)/shard_map/all_to_all | solution.py:37
  759.9 4.9 all-to-all-start.15
  775.7 13.7 all-to-all-done.15
  807.7 13.2 all-to-all-done.14
  883.3 11.1 reduce-scatter.5.cloned.1.call-done
  897.3 49.9 %all-reduce.27.cloned.1.call-done = bf16[4096,128]{1,0:T(8,128)(2,1)} async-done(((bf16[4096,128]{1,0:T(8,128)(2,1)}), bf16[4096,128]{1,0:T(8,128)(2,1)}) %all-reduce.27.cloned.1.call-update) | async-done | bytes 1048592 | tf_op jit(solution)/shard_map/psum | solution.py:101
  992.8 40.3 %all-reduce.29.cloned.1.call-done = bf16[4096,128]{1,0:T(8,128)(2,1)} async-done(((bf16[4096,128]{1,0:T(8,128)(2,1)}), bf16[4096,128]{1,0:T(8,128)(2,1)}) %all-reduce.29.cloned.1.call-update) | async-done | bytes 1048592 | tf_op jit(solution)/shard_map/psum | solution.py:101
  1057.8 10.4 all-to-all-done.19
  1072.7 5.4 fusion.11
  1084.5 13.2 all-to-all-done.17
  1132.4 28.9 %all-reduce.31.cloned.1.call-done = bf16[4096,128]{1,0:T(8,128)(2,1)} async-done(((bf16[4096,128]{1,0:T(8,128)(2,1)}), bf16[4096,128]{1,0:T(8,128)(2,1)}) %all-reduce.31.cloned.1.call-update) | async-done | bytes 1048592 | tf_op jit(solution)/shard_map/psum | solution.py:101
  1203.2 19.5 %all-reduce.33.cloned.1.call-done = bf16[4096,128]{1,0:T(8,128)(2,1)} async-done(((bf16[4096,128]{1,0:T(8,128)(2,1)}), bf16[4096,128]{1,0:T(8,128)(2,1)}) %all-reduce.33.cloned.1.call-update) | async-done | bytes 1048592 | tf_op jit(solution)/shard_map/psum | solution.py:101
  1230.5 5.6 add_convert_fusion.4
  1245.0 11.3 all-to-all-done.20
  1267.8 18.0 all-to-all-done.22
  1329.4 26.6 %all-reduce.35.cloned.1.call-done = bf16[4096,128]{1,0:T(8,128)(2,1)} async-done(((bf16[4096,128]{1,0:T(8,128)(2,1)}), bf16[4096,128]{1,0:T(8,128)(2,1)}) %all-reduce.35.cloned.1.call-update) | async-done | bytes 1048592 | tf_op jit(solution)/shard_map/psum | solution.py:101
  1402.6 39.2 %all-reduce.37.cloned.1.call-done = bf16[4096,128]{1,0:T(8,128)(2,1)} async-done(((bf16[4096,128]{1,0:T(8,128)(2,1)}), bf16[4096,128]{1,0:T(8,128)(2,1)}) %all-reduce.37.cloned.1.call-update) | async-done | bytes 1048592 | tf_op jit(solution)/shard_map/psum | solution.py:101
  1441.9 4.9 add_convert_fusion.3
  1451.4 4.9 fusion.184
  1466.0 11.2 all-to-all-done.23
  1488.7 18.0 all-to-all-done.25
  1524.2 11.4 all-to-all-done.24
  1545.5 19.2 %all-to-all-done.28 = bf16[8,2,8,64,128]{4,3,2,1,0:T(8,128)(2,1)} async-done(((bf16[8,2,8,64,128]{4,3,2,1,0:T(8,128)(2,1)}), bf16[8,2,8,64,128]{4,3,2,1,0:T(8,128)(2,1)}, u32[]{:S(2)}, u32[]{:S(2)}) %all-to-all-start.28) | async-done | bytes 2097184 | tf_op jit(solution)/shard_map/all_to_all | solution.py:37
  1575.6 17.9 all-to-all-done.33
  1611.7 41.0 %all-reduce.39.cloned.1.call-done = bf16[4096,128]{1,0:T(8,128)(2,1)} async-done(((bf16[4096,128]{1,0:T(8,128)(2,1)}), bf16[4096,128]{1,0:T(8,128)(2,1)}) %all-reduce.39.cloned.1.call-update) | async-done | bytes 1048592 | tf_op jit(solution)/shard_map/psum | solution.py:101
  1662.2 7.4 fusion.156
  1683.6 39.8 %all-reduce.41.cloned.1.call-done = bf16[4096,128]{1,0:T(8,128)(2,1)} async-done(((bf16[4096,128]{1,0:T(8,128)(2,1)}), bf16[4096,128]{1,0:T(8,128)(2,1)}) %all-reduce.41.cloned.1.call-update) | async-done | bytes 1048592 | tf_op jit(solution)/shard_map/psum | solution.py:101
  1744.6 8.4 all-to-all-done.32
  1757.5 6.8 multiply_reduce_fusion.1
  1769.2 13.3 all-to-all-done.34
  1798.0 20.1 %all-to-all-done.26 = bf16[4,2,1024,128]{3,2,1,0:T(8,128)(2,1)} async-done(((bf16[4,2,1024,128]{3,2,1,0:T(8,128)(2,1)}), bf16[4,2,1024,128]{3,2,1,0:T(8,128)(2,1)}, u32[]{:S(2)}, u32[]{:S(2)}) %all-to-all-start.26) | async-done | bytes 2097184 | tf_op jit(solution)/shard_map/all_to_all | solution.py:37
  1837.4 34.1 %all-to-all-done.30 = bf16[8,2,8,64,128]{4,3,2,1,0:T(8,128)(2,1)} async-done(((bf16[8,2,8,64,128]{4,3,2,1,0:T(8,128)(2,1)}), bf16[8,2,8,64,128]{4,3,2,1,0:T(8,128)(2,1)}, u32[]{:S(2)}, u32[]{:S(2)}) %all-to-all-start.30) | async-done | bytes 2097184 | tf_op jit(solution)/shard_map/all_to_all | solution.py:37
  (943 shorter events, 790.6 us)
Async XLA Ops:
  96.7 87.1 %all-to-all-start = ((bf16[8,2,8,64,128]{4,3,2,1,0:T(8,128)(2,1)}), bf16[8,2,8,64,128]{4,3,2,1,0:T(8,128)(2,1)}, u32[]{:S(2)}, u32[]{:S(2)}) async-start(bf16[8,2,8,64,128]{4,3,2,1,0:T(8,128)(2,1)} %copy.386), calls=%async_computation | async-start | bytes 4194304 | tf_op jit(solution)/shard_map/all_to_all | solution.py:37
  101.3 203.3 %all-gather.4.cloned.1.call-start = ((), (), s32[]{:S(2)}) async-start(), calls=%async_computation.37 | async-start | bytes 4718592 | tf_op jit(solution)/shard_map/all_gather | solution.py:60
  213.9 49.1 %all-to-all-start.5 = ((bf16[16,256,256]{2,1,0:T(8,128)(2,1)}), bf16[16,256,256]{2,1,0:T(8,128)(2,1)S(1)}, u32[]{:S(2)}, u32[]{:S(2)}) async-start(bf16[16,256,256]{2,1,0:T(8,128)(2,1)} %bitcast.874), calls=%async_computation.5 | async-start | bytes 4194304 | tf_op jit(solution)/shard_map/all_to_all | solution.py:37
  265.0 30.2 %all-to-all-start.4 = ((bf16[8,2,8,64,128]{4,3,2,1,0:T(8,128)(2,1)}), bf16[8,2,8,64,128]{4,3,2,1,0:T(8,128)(2,1)}, u32[]{:S(2)}, u32[]{:S(2)}) async-start(bf16[8,2,8,64,128]{4,3,2,1,0:T(8,128)(2,1)} %bitcast.880), calls=%async_computation.4 | async-start | bytes 4194304 | tf_op jit(solution)/shard_map/all_to_all | solution.py:37
  297.1 29.5 %all-to-all-start.7 = ((bf16[8,2,8,64,128]{4,3,2,1,0:T(8,128)(2,1)}), bf16[8,2,8,64,128]{4,3,2,1,0:T(8,128)(2,1)}, u32[]{:S(2)}, u32[]{:S(2)}) async-start(bf16[8,2,8,64,128]{4,3,2,1,0:T(8,128)(2,1)} %bitcast.871), calls=%async_computation.7 | async-start | bytes 4194304 | tf_op jit(solution)/shard_map/all_to_all | solution.py:37
  329.2 28.9 %all-to-all-start.8 = ((bf16[16,256,256]{2,1,0:T(8,128)(2,1)}), bf16[16,256,256]{2,1,0:T(8,128)(2,1)}, u32[]{:S(2)}, u32[]{:S(2)}) async-start(bf16[16,256,256]{2,1,0:T(8,128)(2,1)} %bitcast.872), calls=%async_computation.8 | async-start | bytes 4194304 | tf_op jit(solution)/shard_map/all_to_all | solution.py:37
  333.6 63.2 %all-reduce.15.cloned.1.call-start = ((), (), s32[]{:S(2)}) async-start(), calls=%async_computation.38 | async-start | bytes 2097152 | tf_op jit(solution)/shard_map/psum | solution.py:101
  359.6 37.3 %all-to-all-start.9 = ((bf16[16,256,256]{2,1,0:T(8,128)(2,1)}), bf16[16,256,256]{2,1,0:T(8,128)(2,1)}, u32[]{:S(2)}, u32[]{:S(2)}) async-start(bf16[16,256,256]{2,1,0:T(8,128)(2,1)} %bitcast.45), calls=%async_computation.9 | async-start | bytes 4194304 | tf_op jit(solution)/shard_map/all_to_all | solution.py:37
  364.1 107.9 %all-reduce.17.cloned.1.call-start = ((), (), s32[]{:S(2)}) async-start(), calls=%async_computation.39 | async-start | bytes 2097152 | tf_op jit(solution)/shard_map/psum | solution.py:101
  474.9 30.7 %all-to-all-start.10 = ((bf16[8,2,8,64,128]{4,3,2,1,0:T(8,128)(2,1)}), bf16[8,2,8,64,128]{4,3,2,1,0:T(8,128)(2,1)}, u32[]{:S(2)}, u32[]{:S(2)}) async-start(bf16[8,2,8,64,128]{4,3,2,1,0:T(8,128)(2,1)} %bitcast.875), calls=%async_computation.10 | async-start | bytes 4194304 | tf_op jit(solution)/shard_map/all_to_all | solution.py:37
  508.2 29.5 %all-to-all-start.11 = ((bf16[16,256,256]{2,1,0:T(8,128)(2,1)}), bf16[16,256,256]{2,1,0:T(8,128)(2,1)}, u32[]{:S(2)}, u32[]{:S(2)}) async-start(bf16[16,256,256]{2,1,0:T(8,128)(2,1)} %bitcast.878), calls=%async_computation.11 | async-start | bytes 4194304 | tf_op jit(solution)/shard_map/all_to_all | solution.py:37
  512.6 62.7 %all-reduce.19.cloned.1.call-start = ((), (), s32[]{:S(2)}) async-start(), calls=%async_computation.40 | async-start | bytes 2097152 | tf_op jit(solution)/shard_map/psum | solution.py:101
  539.2 36.1 %all-to-all-start.12 = ((bf16[16,256,256]{2,1,0:T(8,128)(2,1)}), bf16[16,256,256]{2,1,0:T(8,128)(2,1)}, u32[]{:S(2)}, u32[]{:S(2)}) async-start(bf16[16,256,256]{2,1,0:T(8,128)(2,1)} %bitcast.876), calls=%async_computation.12 | async-start | bytes 4194304 | tf_op jit(solution)/shard_map/all_to_all | solution.py:37
  543.7 105.0 %all-reduce.21.cloned.1.call-start = ((), (), s32[]{:S(2)}) async-start(), calls=%async_computation.41 | async-start | bytes 2097152 | tf_op jit(solution)/shard_map/psum | solution.py:101
  597.3 127.2 %all-reduce.23.cloned.1.call-start = ((), (), s32[]{:S(2)}) async-start(), calls=%async_computation.42 | async-start | bytes 2097152 | tf_op jit(solution)/shard_map/psum | solution.py:101
  673.1 157.4 %all-reduce.25.cloned.1.call-start = ((), (), s32[]{:S(2)}) async-start(), calls=%async_computation.43 | async-start | bytes 2097152 | tf_op jit(solution)/shard_map/psum | solution.py:101
  727.4 29.9 %all-to-all-start.13 = ((bf16[8,2,8,64,128]{4,3,2,1,0:T(8,128)(2,1)}), bf16[8,2,8,64,128]{4,3,2,1,0:T(8,128)(2,1)}, u32[]{:S(2)}, u32[]{:S(2)}) async-start(bf16[8,2,8,64,128]{4,3,2,1,0:T(8,128)(2,1)} %bitcast.877), calls=%async_computation.13 | async-start | bytes 4194304 | tf_op jit(solution)/shard_map/all_to_all | solution.py:37
  731.9 98.8 %all-gather.6.cloned.1.call-start = ((), (), s32[]{:S(2)}) async-start(), calls=%async_computation.45 | async-start | bytes 4718592 | tf_op jit(solution)/shard_map/all_gather | solution.py:60
  734.1 36.0 %collective-permute-start.10 = (bf16[4,1024,128]{2,1,0:T(8,128)(2,1)}, bf16[4,1024,128]{2,1,0:T(8,128)(2,1)}, u32[]{:S(2)}, u32[]{:S(2)}) collective-permute-start(bf16[4,1024,128]{2,1,0:T(8,128)(2,1)} %bitcast.1027), channel_id=1, source_target_pairs={{0,1},{1,0},{2,3},{3,2},{4,5},{5,4},{6,7},{7,6},{8,9},{9,8},{10,11... | collective-permute-start | bytes 3145736 | tf_op jit(solution)/shard_map/ppermute | solution.py:87
  759.9 29.4 %all-to-all-start.15 = ((bf16[16,256,256]{1,2,0:T(8,128)(2,1)}), bf16[16,256,256]{1,2,0:T(8,128)(2,1)}, u32[]{:S(2)}, u32[]{:S(2)}) async-start(bf16[16,256,256]{1,2,0:T(8,128)(2,1)} %bitcast.873), calls=%async_computation.15 | async-start | bytes 4194304 | tf_op jit(solution)/shard_map/all_to_all | solution.py:37
  791.9 28.9 %all-to-all-start.14 = ((bf16[16,256,256]{1,2,0:T(8,128)(2,1)}), bf16[16,256,256]{1,2,0:T(8,128)(2,1)}, u32[]{:S(2)}, u32[]{:S(2)}) async-start(bf16[16,256,256]{1,2,0:T(8,128)(2,1)} %bitcast.879), calls=%async_computation.14 | async-start | bytes 4194304 | tf_op jit(solution)/shard_map/all_to_all | solution.py:37
  796.4 72.5 %reduce-scatter.3.cloned.1.call-start = ((), (), s32[]{:S(2)}) async-start(), calls=%async_computation.44 | async-start | bytes 1310720 | tf_op jit(solution)/shard_map/reduce_scatter | solution.py:99
  837.6 56.7 %reduce-scatter.5.cloned.1.call-start = ((), (), s32[]{:S(2)}) async-start(), calls=%async_computation.46 | async-start | bytes 1310720 | tf_op jit(solution)/shard_map/reduce_scatter | solution.py:99
  868.9 78.3 %all-reduce.27.cloned.1.call-start = ((), (), s32[]{:S(2)}) async-start(), calls=%async_computation.47 | async-start | bytes 2097152 | tf_op jit(solution)/shard_map/psum | solution.py:101
  894.4 138.7 %all-reduce.29.cloned.1.call-start = ((), (), s32[]{:S(2)}) async-start(), calls=%async_computation.48 | async-start | bytes 2097152 | tf_op jit(solution)/shard_map/psum | solution.py:101
  1037.6 30.6 %all-to-all-start.19 = ((bf16[16,256,256]{2,1,0:T(8,128)(2,1)}), bf16[16,256,256]{2,1,0:T(8,128)(2,1)}, u32[]{:S(2)}, u32[]{:S(2)}) async-start(bf16[16,256,256]{2,1,0:T(8,128)(2,1)} %add_convert_fusion.6), calls=%async_computation.21 | async-start | bytes 4194304 | tf_op jit(solution)/shard_map/all_to_all | solution.py:37
  1068.2 29.5 %all-to-all-start.17 = ((bf16[8,2,8,64,128]{4,3,2,1,0:T(8,128)(2,1)}), bf16[8,2,8,64,128]{4,3,2,1,0:T(8,128)(2,1)}, u32[]{:S(2)}, u32[]{:S(2)}) async-start(bf16[8,2,8,64,128]{4,3,2,1,0:T(8,128)(2,1)} %pad_maximum_fusion.2), calls=%async_computation.19 | async-start | bytes 4194304 | tf_op jit(solution)/shard_map/all_to_all | solution.py:37
  1097.7 28.9 %all-to-all-start.18 = ((bf16[16,256,256]{2,1,0:T(8,128)(2,1)}), bf16[16,256,256]{2,1,0:T(8,128)(2,1)}, u32[]{:S(2)}, u32[]{:S(2)}) async-start(bf16[16,256,256]{2,1,0:T(8,128)(2,1)} %add_convert_fusion.7), calls=%async_computation.20 | async-start | bytes 4194304 | tf_op jit(solution)/shard_map/all_to_all | solution.py:37
  1102.2 59.1 %all-reduce.31.cloned.1.call-start = ((), (), s32[]{:S(2)}) async-start(), calls=%async_computation.49 | async-start | bytes 2097152 | tf_op jit(solution)/shard_map/psum | solution.py:101
  1109.2 113.5 %all-reduce.33.cloned.1.call-start = ((), (), s32[]{:S(2)}) async-start(), calls=%async_computation.50 | async-start | bytes 2097152 | tf_op jit(solution)/shard_map/psum | solution.py:101
  1225.8 30.5 %all-to-all-start.20 = ((bf16[8,2,8,64,128]{4,3,2,1,0:T(8,128)(2,1)}), bf16[8,2,8,64,128]{4,3,2,1,0:T(8,128)(2,1)}, u32[]{:S(2)}, u32[]{:S(2)}) async-start(bf16[8,2,8,64,128]{4,3,2,1,0:T(8,128)(2,1)} %pad_maximum_fusion.3), calls=%async_computation.22 | async-start | bytes 4194304 | tf_op jit(solution)/shard_map/all_to_all | solution.py:37
  1256.3 29.5 %all-to-all-start.22 = ((bf16[16,256,256]{2,1,0:T(8,128)(2,1)}), bf16[16,256,256]{2,1,0:T(8,128)(2,1)}, u32[]{:S(2)}, u32[]{:S(2)}) async-start(bf16[16,256,256]{2,1,0:T(8,128)(2,1)} %add_convert_fusion.4), calls=%async_computation.24 | async-start | bytes 4194304 | tf_op jit(solution)/shard_map/all_to_all | solution.py:37
  1290.3 65.8 %all-reduce.35.cloned.1.call-start = ((), (), s32[]{:S(2)}) async-start(), calls=%async_computation.51 | async-start | bytes 2097152 | tf_op jit(solution)/shard_map/psum | solution.py:101
  1314.7 132.0 %all-to-all-start.16 = ((bf16[4,2,1024,128]{3,2,1,0:T(8,128)(2,1)}), bf16[4,2,1024,128]{3,2,1,0:T(8,128)(2,1)}, u32[]{:S(2)}, u32[]{:S(2)}) async-start(bf16[4,2,1024,128]{3,2,1,0:T(8,128)(2,1)} %pad_maximum_fusion.1), calls=%async_computation.18 | async-start | bytes 4194304 | tf_op jit(solution)/shard_map/all_to_all | solution.py:37
  1319.2 122.6 %all-reduce.37.cloned.1.call-start = ((), (), s32[]{:S(2)}) async-start(), calls=%async_computation.52 | async-start | bytes 2097152 | tf_op jit(solution)/shard_map/psum | solution.py:101
  1446.7 30.5 %all-to-all-start.23 = ((bf16[8,2,8,64,128]{4,3,2,1,0:T(8,128)(2,1)}), bf16[8,2,8,64,128]{4,3,2,1,0:T(8,128)(2,1)}, u32[]{:S(2)}, u32[]{:S(2)}) async-start(bf16[8,2,8,64,128]{4,3,2,1,0:T(8,128)(2,1)} %pad_maximum_fusion.4), calls=%async_computation.25 | async-start | bytes 4194304 | tf_op jit(solution)/shard_map/all_to_all | solution.py:37
  1477.2 29.5 %all-to-all-start.25 = ((bf16[16,256,256]{2,1,0:T(8,128)(2,1)}), bf16[16,256,256]{2,1,0:T(8,128)(2,1)}, u32[]{:S(2)}, u32[]{:S(2)}) async-start(bf16[16,256,256]{2,1,0:T(8,128)(2,1)} %add_convert_fusion.2), calls=%async_computation.27 | async-start | bytes 4194304 | tf_op jit(solution)/shard_map/all_to_all | solution.py:37
  1506.7 28.9 %all-to-all-start.24 = ((bf16[16,256,256]{2,1,0:T(8,128)(2,1)}), bf16[16,256,256]{2,1,0:T(8,128)(2,1)}, u32[]{:S(2)}, u32[]{:S(2)}) async-start(bf16[16,256,256]{2,1,0:T(8,128)(2,1)} %add_convert_fusion.3), calls=%async_computation.26 | async-start | bytes 4194304 | tf_op jit(solution)/shard_map/all_to_all | solution.py:37
  1535.6 29.1 %all-to-all-start.28 = ((bf16[8,2,8,64,128]{4,3,2,1,0:T(8,128)(2,1)}), bf16[8,2,8,64,128]{4,3,2,1,0:T(8,128)(2,1)}, u32[]{:S(2)}, u32[]{:S(2)}) async-start(bf16[8,2,8,64,128]{4,3,2,1,0:T(8,128)(2,1)} %pad_maximum_fusion.6), calls=%async_computation.30 | async-start | bytes 4194304 | tf_op jit(solution)/shard_map/all_to_all | solution.py:37
  1564.7 28.9 %all-to-all-start.33 = ((bf16[16,256,256]{2,1,0:T(8,128)(2,1)}), bf16[16,256,256]{2,1,0:T(8,128)(2,1)}, u32[]{:S(2)}, u32[]{:S(2)}) async-start(bf16[16,256,256]{2,1,0:T(8,128)(2,1)} %add_convert_fusion), calls=%async_computation.35 | async-start | bytes 4194304 | tf_op jit(solution)/shard_map/all_to_all | solution.py:37
  1593.6 64.1 %all-to-all-start.31 = ((bf16[16,256,256]{2,1,0:T(8,128)(2,1)}), bf16[16,256,256]{2,1,0:T(8,128)(2,1)}, u32[]{:S(2)}, u32[]{:S(2)}) async-start(bf16[16,256,256]{2,1,0:T(8,128)(2,1)} %add_convert_fusion.1), calls=%async_computation.33 | async-start | bytes 4194304 | tf_op jit(solution)/shard_map/all_to_all | solution.py:37
  1598.0 54.7 %all-reduce.39.cloned.1.call-start = ((), (), s32[]{:S(2)}) async-start(), calls=%async_computation.53 | async-start | bytes 2097152 | tf_op jit(solution)/shard_map/psum | solution.py:101
  1657.6 65.8 %all-to-all-start.29 = ((bf16[4,2,2,8,64,128]{5,4,3,1,2,0:T(8,128)(2,1)}), bf16[4,2,2,8,64,128]{5,4,3,1,2,0:T(8,128)(2,1)}, u32[]{:S(2)}, u32[]{:S(2)}) async-start(bf16[4,2,2,8,64,128]{5,4,3,1,2,0:T(8,128)(2,1)} %pad_maximum_fusion.7), calls=%async_computation.31 | async-start | bytes 4194304 | tf_op jit(solution)/shard_map/all_to_all | solution.py:37
  1662.1 61.3 %all-reduce.41.cloned.1.call-start = ((), (), s32[]{:S(2)}) async-start(), calls=%async_computation.54 | async-start | bytes 2097152 | tf_op jit(solution)/shard_map/psum | solution.py:101
  1676.2 60.3 %collective-permute-start.28 = (bf16[4,1024,128]{2,1,0:T(8,128)(2,1)}, bf16[4,1024,128]{2,1,0:T(8,128)(2,1)}, u32[]{:S(2)}, u32[]{:S(2)}) collective-permute-start(bf16[4,1024,128]{2,1,0:T(8,128)(2,1)} %bitcast.296), channel_id=1, source_target_pairs={{0,1},{1,0},{2,3},{3,2},{4,5},{5,4},{6,7},{7,6},{8,9},{9,8},{10,11... | collective-permute-start | bytes 3145736 | tf_op jit(solution)/shard_map/ppermute | solution.py:87
  1723.4 29.6 %all-to-all-start.32 = ((bf16[4,4,256,256]{3,2,1,0:T(8,128)(2,1)}), bf16[4,4,256,256]{3,2,1,0:T(8,128)(2,1)S(1)}, u32[]{:S(2)}, u32[]{:S(2)}) async-start(bf16[4,4,256,256]{3,2,1,0:T(8,128)(2,1)} %pad_maximum_fusion.8), calls=%async_computation.34 | async-start | bytes 4194304 | tf_op jit(solution)/shard_map/all_to_all | solution.py:37
  1753.0 29.4 %all-to-all-start.34 = ((bf16[4,4,256,256]{3,2,1,0:T(8,128)(2,1)}), bf16[4,4,256,256]{3,2,1,0:T(8,128)(2,1)}, u32[]{:S(2)}, u32[]{:S(2)}) async-start(bf16[4,4,256,256]{3,2,1,0:T(8,128)(2,1)} %pad_maximum_fusion.9), calls=%async_computation.36 | async-start | bytes 4194304 | tf_op jit(solution)/shard_map/all_to_all | solution.py:37
  1818.1 53.4 %all-to-all-start.30 = ((bf16[8,2,8,64,128]{4,3,2,1,0:T(8,128)(2,1)}), bf16[8,2,8,64,128]{4,3,2,1,0:T(8,128)(2,1)}, u32[]{:S(2)}, u32[]{:S(2)}) async-start(bf16[8,2,8,64,128]{4,3,2,1,0:T(8,128)(2,1)} %bitcast.901), calls=%async_computation.32 | async-start | bytes 4194304 | tf_op jit(solution)/shard_map/all_to_all | solution.py:37
  (264 other events, 2172.1 us)
Sparse Core Ops, SparseCore 0:
  104.6 80.9 all-gather.3
  346.4 50.3 all-reduce.14
  420.7 51.2 all-reduce.16
  523.5 51.7 all-reduce.18
  597.5 51.2 all-reduce.20
  673.2 51.2 all-reduce.22
  727.6 51.1 all-reduce.24
  780.4 46.5 all-gather.5
  837.8 25.2 reduce-scatter.2
  869.0 25.2 reduce-scatter.4
  896.7 50.4 all-reduce.26
  981.8 51.2 all-reduce.28
  1109.3 51.8 all-reduce.30
  1171.4 51.2 all-reduce.32
  1304.2 51.8 all-reduce.34
  1390.5 51.2 all-reduce.36
  1600.9 51.7 all-reduce.38
  1671.7 51.6 all-reduce.40
